TPU v7x, 256 devices: a whole 4x4x8 slice. The times are simulated.
256 devices in a mesh: tm: 4 (over y), space: 64 (over x, z, core).
Axes of the slice: x: 4, y: 4, z: 8, core: 2. Of those that a mesh axis runs over, the one named last changes fastest.
Arguments:
- initial_state: float32 [3, 128, 128, 128], P(None, 'space'), may hold values from -6 to 6
- end_states: float32 [4, 3, 128, 128, 128], P('tm', None, 'space'), may hold values from -6 to 6
- old_tendencies: float32 [4, 3, 3, 128, 128, 128], P('tm', None, None, 'space'), may hold values from -6 to 6
Outputs:
- node_states: float32 [4, 3, 3, 128, 128, 128], P('tm', None, None, 'space')
- q_field: float32 [4, 128, 128, 128], P('tm', 'space')
All inputs are finite; a program needn't handle non-finite values.
Results may differ from a plain program's by a relative error of at most 0.00014.
Values sent between devices are 32-bit elements; how exact they have to be, the bound alone decides.
A program may use at most 128 MiB of HBM per device.

v0:
```python
import math

import jax
import jax.numpy as jnp
import numpy as np
from jax import lax
from jax.experimental import pallas as pl
from jax.experimental.pallas import tpu as pltpu
from jax.sharding import PartitionSpec as P

DT = 0.4
HALF = 0.2
NU = 0.1
PARTS = 64
ROWS = 4
N = 128
M = 64
FINE = 12
COARSE = 3
f32 = jnp.float32
MESH = pl.DeviceIdType.MESH


def angle_tables(left, right, count):
    angles = (2.0 * math.pi / count) * (np.outer(left, right) % count)
    return np.cos(angles), np.sin(angles)


def restriction_table(count):
    cos_c, sin_c = angle_tables(np.arange(count // 2), np.arange(count // 4), count // 2)
    cos_f, sin_f = angle_tables(np.arange(count), np.arange(count // 4), count)
    weight = np.where(np.arange(count // 4) == 0, 1.0, 2.0)
    return ((cos_c * weight) @ cos_f.T + (sin_c * weight) @ sin_f.T) / count


def twice(block):
    zero = np.zeros_like(block)
    return np.block([[block, zero], [zero, block]])


def wave_symbols(ids, count, spacing):
    theta = 2.0 * math.pi * ids / count
    kappa = theta / spacing
    first = (8.0 * np.sin(theta) - np.sin(2.0 * theta)) / (6.0 * spacing)
    second = (-2.0 * np.cos(2.0 * theta) + 32.0 * np.cos(theta) - 30.0) / (12.0 * spacing**2)
    return kappa, first, second


def signed(ids, count):
    return np.where(ids < count // 2, ids, ids - count)


def build_tables():
    t = {}
    grid = np.arange(N)
    owner = np.concatenate([2 * np.arange(PARTS), 2 * np.arange(PARTS) + 1])
    cos_y, sin_y = angle_tables(grid, np.arange(M), N)
    t["f_y"] = np.hstack([cos_y, -sin_y, -sin_y, -cos_y])
    t["f_x"] = np.hstack(angle_tables(owner, grid, N))
    t["f_z"] = np.hstack(angle_tables(grid, owner, N))
    t["i_z"] = np.hstack(angle_tables(owner, grid, N))
    t["i_x"] = np.hstack(angle_tables(grid, owner, N))
    weight = np.where(np.arange(M) == 0, 1.0, 2.0) / float(N**3)
    wc, ws = (cos_y * weight).T, (sin_y * weight).T
    t["i_y"] = np.hstack([np.vstack([wc, -ws]), np.vstack([-ws, -wc])])
    half = np.arange(M // 2)
    cos_y, sin_y = angle_tables(np.arange(M), half, M)
    t["cf_y"] = np.hstack([twice(np.hstack([cos_y, -sin_y])), twice(np.hstack([-sin_y, -cos_y]))])
    t["c_x"] = np.hstack(angle_tables(np.arange(M), np.arange(M), M))
    weight = np.where(half == 0, 1.0, 2.0) / float(M * M * N)
    wc, ws = (cos_y * weight).T, (sin_y * weight).T
    t["ci_y"] = np.hstack([twice(np.vstack([wc, -ws])), twice(np.vstack([-ws, -wc]))])
    table = restriction_table(N)
    t["r_x"] = table
    t["r_y"] = twice(table.T)
    t["p_x"] = 4.0 * table.T
    t["p_y"] = twice(table)
    kx, _, _ = wave_symbols(signed(grid, N), N, 1.0)
    ky = np.tile(kx[:M], 2)[None, :]
    ones = np.ones((1, N))
    t["f_kx"] = kx[:, None] * ones
    t["f_mx"] = (grid != M)[:, None] * ones
    t["f_ky"] = np.repeat(ky, 8, axis=0)
    t["f_kz"] = kx[:, None] * ones
    t["f_kk"] = ky**2 + kx[:, None] ** 2
    t["f_mz"] = t["f_mx"]
    ckx, sx, lx = wave_symbols(signed(np.arange(M), M), M, 2.0)
    t["c_kx"] = ckx[:, None] * ones
    t["c_mx"] = (np.arange(M) != M // 2)[:, None] * ones
    t["c_sx"] = sx[:, None] * ones
    t["c_lx"] = lx[:, None] * ones
    lane = lambda v: np.tile(v[: M // 2], 4)[None, :]
    cky, sy, ly = lane(ckx), lane(sx), lane(lx)
    zid = np.hstack([np.repeat(np.arange(M)[:, None], M, 1), np.repeat(np.arange(M)[:, None] + M, M, 1)])
    ckz, sz, lz = wave_symbols(signed(zid, N), N, 1.0)
    t["c_ky"] = np.repeat(cky, 8, axis=0)
    t["c_sy"] = np.repeat(sy, 8, axis=0)
    t["c_kz"] = ckz
    t["c_sz"] = sz
    t["c_kk"] = cky**2 + ckz**2
    t["c_mz"] = (zid != M) * 1.0
    t["c_ll"] = ly + lz
    turn = 2.0 * math.pi * np.arange(M)[:, None] / N
    first = (np.arange(N) < M)[None, :]
    t["tw_c"] = np.where(first, 1.0, np.cos(turn))
    t["tw_s"] = np.where(first, 0.0, np.sin(turn))
    made = {}
    for name, value in t.items():
        value = np.asarray(value, np.float32)
        if name in SPLIT:
            high = value.astype(jnp.bfloat16)
            made[name + "_h"] = high
            made[name + "_l"] = (value - high.astype(np.float32)).astype(jnp.bfloat16)
        else:
            made[name] = value
    return made


SPLIT = ("f_x", "f_y", "f_z", "i_x", "i_y", "i_z", "cf_y", "c_x", "ci_y")
TABLES = build_tables()
NAMES = tuple(sorted(TABLES))


def exact(a, b):
    return jnp.dot(a, b, precision=lax.Precision.HIGHEST, preferred_element_type=f32)


def dot(a, b):
    return jnp.dot(a, b, preferred_element_type=f32)


def split(x):
    high = x.astype(jnp.bfloat16)
    return high, (x - high.astype(f32)).astype(jnp.bfloat16)


def by_table(x, t, name):
    high, low = split(x)
    table = t[name + "_h"][...]
    return dot(high, table) + (dot(low, table) + dot(high, t[name + "_l"][...]))


def table_by(t, name, x):
    high, low = split(x)
    table = t[name + "_h"][...]
    return dot(table, high) + (dot(table, low) + dot(t[name + "_l"][...], high))


def roll(x, shift, axis):
    return pltpu.roll(x, shift % x.shape[axis], axis)


def lanes(shape):
    return lax.broadcasted_iota(jnp.int32, shape, 1)


def stacked(a, b):
    return jnp.concatenate([a, b], axis=0)


def both_halves(wide):
    return stacked(wide[:, :N], wide[:, N:])


def turn_back(x):
    swapped = roll(x, M, 1)
    return jnp.where(lanes(x.shape) < M, swapped, -swapped)


def turn_back_c(x):
    is_real = (lanes(x.shape) % M) < M // 2
    return jnp.where(is_real, roll(x, -M // 2, 1), -roll(x, M // 2, 1))


def butterfly(x):
    return jnp.where(lanes(x.shape) < M, x, -x) + roll(x, M, 1)


def cross(a, b):
    return (
        a[1] * b[2] - a[2] * b[1],
        a[2] * b[0] - a[0] * b[2],
        a[0] * b[1] - a[1] * b[0],
    )


def first_fine(f, axis):
    return (roll(f, 2, axis) - roll(f, -2, axis) + 8.0 * (roll(f, -1, axis) - roll(f, 1, axis))) * (
        1.0 / 12.0
    )


def second_fine_xy(f):
    near = (roll(f, 1, 0) + roll(f, -1, 0)) + (roll(f, 1, 1) + roll(f, -1, 1))
    far = (roll(f, 2, 0) + roll(f, -2, 0)) + (roll(f, 2, 1) + roll(f, -2, 1))
    return (16.0 * near - far - 60.0 * f) * (1.0 / 12.0)


def roll_half(f, shift):
    place = lanes(f.shape) % M
    keep = place >= shift if shift > 0 else place < M + shift
    return jnp.where(keep, roll(f, shift, 1), roll(f, shift - M if shift > 0 else shift + M, 1))


def first_coarse(f, along_x):
    go = (lambda s: roll(f, s, 0)) if along_x else (lambda s: roll_half(f, s))
    return (go(2) - go(-2) + 8.0 * (go(-1) - go(1))) * (1.0 / 24.0)


def second_coarse_xy(f):
    near = (roll(f, 1, 0) + roll(f, -1, 0)) + (roll_half(f, 1) + roll_half(f, -1))
    far = (roll(f, 2, 0) + roll(f, -2, 0)) + (roll_half(f, 2) + roll_half(f, -2))
    return (16.0 * near - far - 60.0 * f) * (1.0 / 48.0)


def first_next(a, b):
    return (a - 8.0 * b) * (1.0 / 12.0), b * (1.0 / 12.0)


def first_prev(a, b):
    return a * (-1.0 / 12.0), (8.0 * a - b) * (1.0 / 12.0)


def first_own(a, b):
    return b * (8.0 / 12.0), a * (-8.0 / 12.0)


def second_next(a, b):
    return (16.0 * b - a) * (1.0 / 12.0), b * (-1.0 / 12.0)


def second_prev(a, b):
    return a * (-1.0 / 12.0), (16.0 * a - b) * (1.0 / 12.0)


def second_own(a, b):
    return (16.0 * b - 30.0 * a) * (1.0 / 12.0), (16.0 * a - 30.0 * b) * (1.0 / 12.0)


def lane_pair(f, low, high):
    is_low = lanes(f.shape) < M
    own = jnp.where(is_low, low[0], high[0]).astype(f32)
    other = jnp.where(is_low, low[1], high[1]).astype(f32)
    return f * own + roll(f, M, 1) * other


T12 = 1.0 / 12.0


def c_first_next(f):
    return lane_pair(f, (T12, -8 * T12), (T12, 0.0))


def c_first_prev(f):
    return lane_pair(f, (-T12, 0.0), (-T12, 8 * T12))


def c_first_own(f):
    return lane_pair(f, (0.0, 8 * T12), (0.0, -8 * T12))


def c_second_next(f):
    return lane_pair(f, (-T12, 16 * T12), (-T12, 0.0))


def c_second_prev(f):
    return lane_pair(f, (-T12, 0.0), (-T12, 16 * T12))


def c_second_own(f):
    return lane_pair(f, (-30 * T12, 16 * T12), (-30 * T12, 16 * T12))


def forward_fine(plane, t):
    return table_by(t, "f_x", both_halves(by_table(plane, t, "f_y")))


def inverse_fine(modes, t):
    return table_by(t, "i_x", both_halves(by_table(modes, t, "i_y")))


def forward_coarse(pair, t):
    return table_by(t, "c_x", both_halves(by_table(pair, t, "cf_y")))


def inverse_coarse(modes, t):
    return table_by(t, "c_x", both_halves(by_table(modes, t, "ci_y")))


def solve_fine(planes, kx, mx, t):
    hat = [table_by(t, "f_z", stacked(p, turn_back(p))) for p in planes]
    kz = t["f_kz"][...]
    ky = jnp.broadcast_to(t["f_ky"][0:1, :], kz.shape)
    squared = t["f_kk"][...] + kx * kx
    live = squared > 0.0
    inverse = jnp.where(live, t["f_mz"][...] * mx / jnp.where(live, squared, 1.0), 0.0)
    out = []
    for r in cross((kx, ky, kz), hat):
        r = r * inverse
        out.append(table_by(t, "i_z", stacked(-turn_back(r), -r)))
    return out


def z_coarse(x, t):
    d = table_by(t, "c_x", stacked(x, turn_back_c(x)))
    return butterfly(t["tw_c"][...] * d + t["tw_s"][...] * turn_back_c(d))


def z_coarse_back(a, t):
    b = butterfly(a)
    b = t["tw_c"][...] * b - t["tw_s"][...] * turn_back_c(b)
    return table_by(t, "c_x", stacked(b, -turn_back_c(b)))


def velocity_modes(hat, kx, mx, t):
    kz = t["c_kz"][...]
    ky = jnp.broadcast_to(t["c_ky"][0:1, :], kz.shape)
    squared = t["c_kk"][...] + kx * kx
    live = squared > 0.0
    inverse = jnp.where(live, t["c_mz"][...] * mx / jnp.where(live, squared, 1.0), 0.0)
    return [-turn_back_c(r * inverse) for r in cross((kx, ky, kz), hat)]


def tendency_modes(flux, w, sx, lx, t):
    sz = t["c_sz"][...]
    sy = jnp.broadcast_to(t["c_sy"][0:1, :], sz.shape)
    spread = NU * (t["c_ll"][...] + lx)
    return [-turn_back_c(r) + spread * w[i] for i, r in enumerate(cross((sx, sy, sz), flux))]


def restrict(a, b, t):
    return exact(t["r_x"][...], exact(jnp.concatenate([a, b], axis=1), t["r_y"][...]))


def prolong(pair, t):
    wide = exact(exact(t["p_x"][...], pair), t["p_y"][...])
    return wide[:, :N], wide[:, N:]


SCRATCH = dict(
    node=pltpu.VMEM((3, 3, 2, N, N), f32),
    speed=pltpu.VMEM((3, 2, N, N), f32),
    flux=pltpu.VMEM((3, 2, N, N), f32),
    total=pltpu.VMEM((3, 2, N, N), f32),
    slope=pltpu.VMEM((3, 2, N, N), f32),
    fs=pltpu.VMEM((6, PARTS * FINE, N), f32),
    fr=pltpu.VMEM((6, PARTS * FINE, N), f32),
    cs=pltpu.VMEM((6, PARTS * COARSE, N), f32),
    cr=pltpu.VMEM((6, PARTS * COARSE, N), f32),
    fh_next=pltpu.VMEM((4, 3, 2, N, N), f32),
    fh_prev=pltpu.VMEM((4, 3, 2, N, N), f32),
    fh_low=pltpu.VMEM((4, 3, 2, N, N), f32),
    fh_high=pltpu.VMEM((4, 3, 2, N, N), f32),
    ch_next=pltpu.VMEM((5, 3, M, N), f32),
    ch_prev=pltpu.VMEM((5, 3, M, N), f32),
    ch_low=pltpu.VMEM((5, 3, M, N), f32),
    ch_high=pltpu.VMEM((5, 3, M, N), f32),
    hand_v=pltpu.VMEM((3, M, N), f32),
    hand_u=pltpu.VMEM((3, M, N), f32),
    hand_m=pltpu.VMEM((3, M, N), f32),
    send_v=pltpu.VMEM((3, M, N), f32),
    send_u=pltpu.VMEM((3, M, N), f32),
    send_m=pltpu.VMEM((3, M, N), f32),
    co=pltpu.VMEM((14, 3, M, N), f32),
    f_ssem=pltpu.SemaphoreType.DMA((6,)),
    f_rsem=pltpu.SemaphoreType.DMA((6,)),
    c_ssem=pltpu.SemaphoreType.DMA((6,)),
    c_rsem=pltpu.SemaphoreType.DMA((6,)),
    h_ssem=pltpu.SemaphoreType.DMA((9, 2)),
    h_rsem=pltpu.SemaphoreType.DMA((9, 2)),
    y_ssem=pltpu.SemaphoreType.DMA((4,)),
    y_rsem=pltpu.SemaphoreType.DMA((4,)),
)
A0, A2, UA0, UA2, G0, G2, C1, C2, CM1, CM2, B1, S1, BM1, SM1 = range(14)


def kernel(*refs):
    count = len(NAMES)
    init, end, old = refs[:3]
    t = dict(zip(NAMES, refs[3 : 3 + count]))
    nodes, q_out = refs[3 + count : 5 + count]
    s = dict(zip(SCRATCH, refs[5 + count :]))
    co = s["co"]
    row = lax.axis_index("tm")
    me = lax.axis_index("space")
    ahead = lax.rem(me + 1, PARTS)
    behind = lax.rem(me + PARTS - 1, PARTS)
    up = lax.rem(row + 1, ROWS)
    down = lax.rem(row + ROWS - 1, ROWS)

    barrier = pltpu.get_barrier_semaphore()

    def greet(k, carry):
        pl.semaphore_signal(barrier, inc=1, device_id=(row, lax.rem(me + k, PARTS)), device_id_type=MESH)
        return carry

    lax.fori_loop(1, PARTS, greet, 0)
    pl.semaphore_signal(barrier, inc=1, device_id=(up, me), device_id_type=MESH)
    pl.semaphore_signal(barrier, inc=1, device_id=(down, me), device_id_type=MESH)
    pl.semaphore_wait(barrier, PARTS + 1)


    def transpose_start(send, recv, depth, ssem, rsem):
        mine = pl.ds(me * depth, depth)
        pltpu.make_async_copy(send.at[mine], recv.at[mine], rsem).start()

        def step(k, carry):
            to = lax.rem(me + k, PARTS)
            pltpu.make_async_remote_copy(
                src_ref=send.at[pl.ds(to * depth, depth)],
                dst_ref=recv.at[mine],
                send_sem=ssem,
                recv_sem=rsem,
                device_id=(row, to),
                device_id_type=MESH,
            ).start()
            return carry

        lax.fori_loop(1, PARTS, step, 0)

    def arrived(ref, sem):
        pltpu.make_async_copy(ref, ref, sem).wait()

    def left(ref, depth, sem):
        part = ref.at[pl.ds(0, (PARTS - 1) * depth)]
        pltpu.make_async_copy(part, part, sem).wait()

    def fine_start(i):
        transpose_start(s["fs"].at[i], s["fr"].at[i], FINE, s["f_ssem"].at[i], s["f_rsem"].at[i])

    def coarse_start(i):
        transpose_start(s["cs"].at[i], s["cr"].at[i], COARSE, s["c_ssem"].at[i], s["c_rsem"].at[i])

    def fine_wait(i):
        arrived(s["fr"].at[i], s["f_rsem"].at[i])

    def coarse_wait(i):
        arrived(s["cr"].at[i], s["c_rsem"].at[i])

    def halo_copies(kind, i, sem):
        return (
            pltpu.make_async_remote_copy(
                src_ref=s[kind + "h_next"].at[i],
                dst_ref=s[kind + "h_low"].at[i],
                send_sem=s["h_ssem"].at[sem, 0],
                recv_sem=s["h_rsem"].at[sem, 0],
                device_id=(row, ahead),
                device_id_type=MESH,
            ),
            pltpu.make_async_remote_copy(
                src_ref=s[kind + "h_prev"].at[i],
                dst_ref=s[kind + "h_high"].at[i],
                send_sem=s["h_ssem"].at[sem, 1],
                recv_sem=s["h_rsem"].at[sem, 1],
                device_id=(row, behind),
                device_id_type=MESH,
            ),
        )

    def halo_start(kind, i, sem):
        for copy in halo_copies(kind, i, sem):
            copy.start()

    def halo_wait(kind, i, sem):
        for copy in halo_copies(kind, i, sem):
            copy.wait_recv()

    def halo_left(kind, i, sem):
        for copy in halo_copies(kind, i, sem):
            copy.wait_send()

    def hand_copy(src, dst, sem):
        return pltpu.make_async_remote_copy(
            src_ref=src,
            dst_ref=dst,
            send_sem=s["y_ssem"].at[sem],
            recv_sem=s["y_rsem"].at[sem],
            device_id=(up, me),
            device_id_type=MESH,
        )

    start_copy = hand_copy(end.at[0], s["node"].at[0], 0)
    v_copy = hand_copy(s["send_v"], s["hand_v"], 1)
    u_copy = hand_copy(s["send_u"], s["hand_u"], 2)
    m_copy = hand_copy(s["send_m"], s["hand_m"], 3)
    is_first = row == 0
    has_next = row < ROWS - 1


    def fine_send(get, i):
        for c in range(3):
            for z in range(2):
                out = forward_fine(get(c, z), t)
                for low in range(2):
                    s["fs"][i, pl.ds((c * 2 + z) * 2 + low, PARTS, stride=FINE), :] = out[low * M : low * M + M]

    def fine_modes(i):
        for low in range(2):
            planes = [
                stacked(
                    s["fr"][i, pl.ds((c * 2) * 2 + low, PARTS, stride=FINE), :],
                    s["fr"][i, pl.ds((c * 2 + 1) * 2 + low, PARTS, stride=FINE), :],
                )
                for c in range(3)
            ]
            at = pl.ds(me * 2 + low, 1)
            kx = jnp.broadcast_to(t["f_kx"][at, :], (N, N))
            mx = jnp.broadcast_to(t["f_mx"][at, :], (N, N))
            for c, out in enumerate(solve_fine(planes, kx, mx, t)):
                for z in range(2):
                    s["fs"][i + 1, pl.ds((c * 2 + z) * 2 + low, PARTS, stride=FINE), :] = out[z * M : z * M + M]

    def fine_velocity(i):
        for c in range(3):
            for z in range(2):
                at = (c * 2 + z) * 2
                modes = stacked(
                    s["fr"][i, pl.ds(at, PARTS, stride=FINE), :],
                    s["fr"][i, pl.ds(at + 1, PARTS, stride=FINE), :],
                )
                s["speed"][c, z] = inverse_fine(modes, t)

    node, speed, flux, total = s["node"], s["speed"], s["flux"], s["total"]

    def fine_flux(m):
        for z in range(2):
            parts = cross([speed[c, z] for c in range(3)], [node[m, c, z] for c in range(3)])
            for c in range(3):
                flux[c, z] = parts[c]
        for c in range(3):
            w0, w1 = node[m, c, 0], node[m, c, 1]
            ahead0, ahead1 = second_next(w0, w1)
            back0, back1 = second_prev(w0, w1)
            ahead0, ahead1, back0, back1 = NU * ahead0, NU * ahead1, NU * back0, NU * back1
            if c < 2:
                sign = -1.0 if c == 0 else 1.0
                g0, g1 = sign * flux[1 - c, 0], sign * flux[1 - c, 1]
                d0, d1 = first_next(g0, g1)
                e0, e1 = first_prev(g0, g1)
                ahead0, ahead1, back0, back1 = ahead0 + d0, ahead1 + d1, back0 + e0, back1 + e1
            s["fh_next"][m, c, 0] = ahead0
            s["fh_next"][m, c, 1] = ahead1
            s["fh_prev"][m, c, 0] = back0
            s["fh_prev"][m, c, 1] = back1
        halo_start("f", m, m)

    def fine_local(m, c):
        w0, w1 = node[m, c, 0], node[m, c, 1]
        own = [NU * v for v in second_own(w0, w1)]
        if c < 2:
            sign = -1.0 if c == 0 else 1.0
            extra = first_own(sign * flux[1 - c, 0], sign * flux[1 - c, 1])
            own = [own[z] + extra[z] for z in range(2)]
        out = []
        for z in range(2):
            if c == 0:
                curl = first_fine(flux[2, z], 1)
            elif c == 1:
                curl = -first_fine(flux[2, z], 0)
            else:
                curl = first_fine(flux[1, z], 0) - first_fine(flux[0, z], 1)
            out.append(curl + NU * second_fine_xy((w0, w1)[z]) + own[z])
        return out


    def coarse_send(values, i):
        for c in range(3):
            s["cs"][i, pl.ds(c, PARTS, stride=COARSE), :] = forward_coarse(values[c], t)

    def coarse_recv(i):
        return [s["cr"][i, pl.ds(c, PARTS, stride=COARSE), :] for c in range(3)]

    def coarse_modes(i):
        return [z_coarse(x, t) for x in coarse_recv(i)]

    def coarse_velocity(i):
        return [inverse_coarse(x, t) for x in coarse_recv(i)]

    mine = pl.ds(me, 1)
    wide = lambda name: jnp.broadcast_to(t[name][mine, :], (M, N))

    def coarse_back(hat, i):
        modes = velocity_modes(hat, wide("c_kx"), wide("c_mx"), t)
        for c in range(3):
            s["cs"][i, pl.ds(c, PARTS, stride=COARSE), :] = z_coarse_back(modes[c], t)

    def coarse_flux(u, w, i):
        f = cross(u, w)
        g = (-f[1], f[0], None)
        for c in range(3):
            nxt, prv = NU * c_second_next(w[c]), NU * c_second_prev(w[c])
            if g[c] is not None:
                nxt, prv = nxt + c_first_next(g[c]), prv + c_first_prev(g[c])
            s["ch_next"][i, c] = nxt
            s["ch_prev"][i, c] = prv
        halo_start("c", i, 4 + i)
        return f

    def coarse_tendency(f, w, i):
        own = [NU * (second_coarse_xy(w[c]) + c_second_own(w[c])) for c in range(3)]
        parts = [
            first_coarse(f[2], False) - c_first_own(f[1]),
            c_first_own(f[0]) - first_coarse(f[2], True),
            first_coarse(f[1], True) - first_coarse(f[0], False),
        ]
        halo_wait("c", i, 4 + i)
        return [own[c] + parts[c] + (s["ch_low"][i, c] + s["ch_high"][i, c]) for c in range(3)]

    def keep(i, values):
        for c in range(3):
            co[i, c] = values[c]

    def kept(i):
        return [co[i, c] for c in range(3)]

    def restricted(get):
        return [restrict(get(c, 0), get(c, 1), t) for c in range(3)]


    @pl.when(has_next)
    def _():
        start_copy.start()

    @pl.when(is_first)
    def _():
        for c in range(3):
            for z in range(2):
                node[0, c, z] = init[c, z]

    @pl.when(jnp.logical_not(is_first))
    def _():
        start_copy.wait_recv()

    f0 = lambda c, z: old[0, 0, c, z]
    f1 = lambda c, z: old[0, 1, c, z]
    f2 = lambda c, z: old[0, 2, c, z]

    for m in range(3):
        fine_send(lambda c, z: node[m, c, z], 2 * m)
        fine_start(2 * m)
        if m == 0:
            keep(A0, restricted(lambda c, z: node[0, c, z]))
        if m == 1:
            keep(UA0, restricted(lambda c, z: speed[c, z]))
            flux_g0 = coarse_flux(kept(UA0), kept(A0), 0)
            keep(G0, coarse_tendency(flux_g0, kept(A0), 0))
        if m == 2:
            keep(A2, restricted(lambda c, z: node[2, c, z]))
        fine_wait(2 * m)
        fine_modes(2 * m)
        fine_start(2 * m + 1)
        fine_wait(2 * m + 1)
        fine_velocity(2 * m + 1)
        fine_flux(m)
        if m == 2:
            keep(UA2, restricted(lambda c, z: speed[c, z]))
            flux_g2 = coarse_flux(kept(UA2), kept(A2), 1)
        weight = (DT / 6.0, DT * 2.0 / 3.0, DT / 6.0)[m]
        if m < 2:
            for c in range(3):
                local = fine_local(m, c)
                for z in range(2):
                    total[c, z] = weight * local[z] if m == 0 else total[c, z] + weight * local[z]
                    if m == 0:
                        old_part = (
                            (DT * 5.0 / 24.0 - HALF) * f0(c, z)
                            + (DT / 3.0) * f1(c, z)
                            - (DT / 24.0) * f2(c, z)
                        )
                    else:
                        old_part = (
                            (-DT / 24.0) * f0(c, z)
                            + (DT / 3.0 - HALF) * f1(c, z)
                            + (DT * 5.0 / 24.0) * f2(c, z)
                        )
                    node[m + 1, c, z] = node[m, c, z] + HALF * local[z] + old_part
            halo_wait("f", m, m)
            for c in range(3):
                for z in range(2):
                    share = s["fh_low"][m, c, z] + s["fh_high"][m, c, z]
                    total[c, z] = total[c, z] + weight * share
                    node[m + 1, c, z] = node[m + 1, c, z] + HALF * share
        else:
            for c in range(3):
                local = fine_local(m, c)
                for z in range(2):
                    total[c, z] = total[c, z] + weight * local[z]
            halo_wait("f", m, m)
            for c in range(3):
                for z in range(2):
                    share = s["fh_low"][m, c, z] + s["fh_high"][m, c, z]
                    total[c, z] = total[c, z] + weight * share

    rest = restricted(lambda c, z: total[c, z])
    keep(C1, [rest[c] + jnp.where(is_first, co[A0, c], -DT * co[G0, c]) for c in range(3)])
    coarse_send(kept(C1), 0)
    coarse_start(0)
    keep(G2, coarse_tendency(flux_g2, kept(A2), 1))
    keep(
        C2,
        [
            rest[c] - HALF * co[G2, c] + jnp.where(is_first, co[A0, c], -HALF * co[G0, c])
            for c in range(3)
        ],
    )
    coarse_send(kept(C2), 1)
    coarse_start(1)

    for c in range(3):
        a, b = speed[c, 0], speed[c, 1]
        s["fh_next"][3, c, 0], s["fh_next"][3, c, 1] = first_next(a, b)
        s["fh_prev"][3, c, 0], s["fh_prev"][3, c, 1] = first_prev(a, b)
    halo_start("f", 3, 3)

    coarse_wait(0)
    keep(CM1, coarse_modes(0))
    sx, lx = wide("c_sx"), wide("c_lx")

    @pl.when(is_first)
    def _():
        keep(BM1, kept(CM1))
        keep(B1, kept(C1))
        keep(S1, kept(C2))
        for c in range(3):
            s["hand_v"][c] = co[A0, c]

    @pl.when(jnp.logical_not(is_first))
    def _():
        coarse_wait(1)
        keep(CM2, coarse_modes(1))
        v_copy.wait_recv()
        u_copy.wait_recv()
        start = [s["hand_v"][c] for c in range(3)]
        f = coarse_flux([s["hand_u"][c] for c in range(3)], start, 2)
        coarse_send(f, 2)
        coarse_start(2)
        early = coarse_tendency(f, start, 2)
        keep(B1, [start[c] + DT * early[c] + co[C1, c] for c in range(3)])
        keep(S1, [start[c] + HALF * early[c] + co[C2, c] for c in range(3)])
        m_copy.wait_recv()
        coarse_wait(2)
        held = [s["hand_m"][c] for c in range(3)]
        early = tendency_modes(coarse_modes(2), held, sx, lx, t)
        keep(BM1, [held[c] + DT * early[c] + co[CM1, c] for c in range(3)])
        keep(SM1, [held[c] + HALF * early[c] + co[CM2, c] for c in range(3)])

    coarse_back(kept(BM1), 3)
    coarse_start(3)

    @pl.when(is_first)
    def _():
        coarse_wait(1)
        keep(SM1, coarse_modes(1))

    coarse_wait(3)
    middle = kept(B1)
    f = coarse_flux(coarse_velocity(3), middle, 3)
    coarse_send(f, 4)
    coarse_start(4)
    later = coarse_tendency(f, middle, 3)
    for c in range(3):
        s["send_v"][c] = co[S1, c] + HALF * later[c]

    @pl.when(has_next)
    def _():
        v_copy.start()

    coarse_wait(4)
    later = tendency_modes(coarse_modes(4), kept(BM1), sx, lx, t)
    for c in range(3):
        s["send_m"][c] = co[SM1, c] + HALF * later[c]
    coarse_back([s["send_m"][c] for c in range(3)], 5)
    coarse_start(5)

    @pl.when(has_next)
    def _():
        m_copy.start()

    for c in range(3):
        zero = prolong(s["hand_v"][c] - co[A0, c], t)
        two = prolong(s["send_v"][c] - co[A2, c], t)
        for z in range(2):
            nodes[0, 0, c, z] = node[0, c, z] + zero[z]
            nodes[0, 1, c, z] = node[1, c, z] + 0.5 * (zero[z] + two[z])
            nodes[0, 2, c, z] = node[2, c, z] + two[z]

    halo_wait("f", 3, 3)
    slope = s["slope"]
    for c in range(3):
        own = first_own(speed[c, 0], speed[c, 1])
        for z in range(2):
            slope[c, z] = own[z] + (s["fh_low"][3, c, z] + s["fh_high"][3, c, z])

    coarse_wait(5)
    out = coarse_velocity(5)
    for c in range(3):
        s["send_u"][c] = out[c]

    @pl.when(has_next)
    def _():
        u_copy.start()

    change = [out[c] - co[UA2, c] for c in range(3)]
    for c in range(3):
        s["ch_next"][4, c] = c_first_next(change[c])
        s["ch_prev"][4, c] = c_first_prev(change[c])
    halo_start("c", 4, 8)
    for c in range(3):
        put = prolong(change[c], t)
        for z in range(2):
            speed[c, z] = speed[c, z] + put[z]
    own = [c_first_own(change[c]) for c in range(3)]
    halo_wait("c", 4, 8)
    for c in range(3):
        put = prolong(own[c] + (s["ch_low"][4, c] + s["ch_high"][4, c]), t)
        for z in range(2):
            slope[c, z] = slope[c, z] + put[z]
    for z in range(2):
        gx = [first_fine(speed[c, z], 0) for c in range(3)]
        gy = [first_fine(speed[c, z], 1) for c in range(3)]
        gz = [slope[c, z] for c in range(3)]
        diagonal = gx[0] * gx[0] + gy[1] * gy[1] + gz[2] * gz[2]
        mixed = gx[1] * gy[0] + gx[2] * gz[0] + gy[2] * gz[1]
        q_out[0, z] = -0.5 * diagonal - mixed

    for i in range(6):
        left(s["fs"].at[i], FINE, s["f_ssem"].at[i])
    for i in (0, 1, 3, 4, 5):
        left(s["cs"].at[i], COARSE, s["c_ssem"].at[i])

    @pl.when(jnp.logical_not(is_first))
    def _():
        left(s["cs"].at[2], COARSE, s["c_ssem"].at[2])
        halo_left("c", 2, 6)

    for i in range(4):
        halo_left("f", i, i)
    for i in (0, 1, 3, 4):
        halo_left("c", i, 4 + i)

    @pl.when(has_next)
    def _():
        for copy in (start_copy, v_copy, u_copy, m_copy):
            copy.wait_send()


def body(initial_state, end_states, old_tendencies):
    vmem = pl.BlockSpec(memory_space=pltpu.VMEM)
    return pl.pallas_call(
        kernel,
        out_shape=(
            jax.ShapeDtypeStruct((1, 3, 3, 2, N, N), f32),
            jax.ShapeDtypeStruct((1, 2, N, N), f32),
        ),
        in_specs=[vmem] * (3 + len(NAMES)),
        out_specs=(vmem, vmem),
        scratch_shapes=list(SCRATCH.values()),
        compiler_params=pltpu.CompilerParams(
            collective_id=0, has_side_effects=True, vmem_limit_bytes=56 * 1024 * 1024
        ),
    )(initial_state, end_states, old_tendencies, *[jnp.asarray(TABLES[name]) for name in NAMES])


def solution(mesh):
    in_specs = (
        P(None, "space", None, None),
        P("tm", None, "space", None, None),
        P("tm", None, None, "space", None, None),
    )
    out_specs = (P("tm", None, None, "space", None, None), P("tm", "space", None, None))
    return jax.shard_map(body, mesh=mesh, in_specs=in_specs, out_specs=out_specs, check_vma=False)
```

profile of v0, /device:TPU:24, one launch (start us, length us, event | category | flops | bytes accessed | tf_op | source)
XLA Modules:
  0.0 269.1 jit_solution(17037817060358918500)
XLA Ops:
  0.6 265.4 %shard_map.419 = (f32[1,3,3,2,128,128]{5,4,3,2,1,0:T(8,128)}, f32[1,2,128,128]{3,2,1,0:T(8,128)}) custom-call(f32[3,2,128,128]{3,2,1,0:T(8,128)} %refs_0_.1, f32[1,3,2,128,128]{4,3,2,1,0:T(8,128)} %refs_1_.1, f32[1,3,3,2,128,128]{5,4,3,2,1,0:T(8,128)} %refs_2_.1, f32[64,128]{1,0:T(8,128)} %constant.70.clone.refs_3_, f32[64,128]{1,0:T(8,128)} %constant.71.clone.refs_4_, ...), custom_call_target="tpu_custom_call" | custom-call | tf_op jit(solution)/shard_map/pallas_call | solution.py:849
  266.0 0.0 copy-start
  266.1 2.4 copy.48
  268.5 0.0 copy-done
  268.5 0.7 copy.49
Async XLA Ops:
  266.0 2.4 copy-start
where the time goes:
time: 269 us
  Pallas kernels  265 us (99%)
  local copies, waits for them, and re-layouts  3.08 us (1%)
    pallas_call x1, Pallas kernels, body(): pl.pallas_call(kernel, out_shape=(jax.ShapeDtypeStruct((1, 3, 3, 2, N, N)...  265 us

commit v1 on v0

--- a/solution.py
+++ b/solution.py
@@ -74,7 +74,7 @@
     t["r_x"] = table
     t["r_y"] = twice(table.T)
     t["p_x"] = 4.0 * table.T
-    t["p_y"] = twice(table)
+    t["p_y0"], t["p_y1"] = np.hsplit(twice(table), 2)
     kx, _, _ = wave_symbols(signed(grid, N), N, 1.0)
     ky = np.tile(kx[:M], 2)[None, :]
     ones = np.ones((1, N))
@@ -118,7 +118,24 @@
 
 SPLIT = ("f_x", "f_y", "f_z", "i_x", "i_y", "i_z", "cf_y", "c_x", "ci_y")
 TABLES = build_tables()
-NAMES = tuple(sorted(TABLES))
+
+
+def pack(kind, width):
+    places, blocks, top = {}, [], 0
+    for name in sorted(TABLES):
+        value = TABLES[name]
+        if value.dtype == kind:
+            block = np.zeros((value.shape[0], width), kind)
+            block[:, : value.shape[1]] = value
+            places[name] = (top, value.shape)
+            blocks.append(block)
+            top += value.shape[0]
+    return places, np.concatenate(blocks)
+
+
+PLACES_32, PACKED_32 = pack(np.float32, N)
+PLACES_16, PACKED_16 = pack(jnp.bfloat16, 2 * N)
+OPERANDS = 5
 
 
 def exact(a, b):
@@ -287,13 +304,16 @@
     return table_by(t, "c_x", both_halves(by_table(modes, t, "ci_y")))
 
 
-def solve_fine(planes, kx, mx, t):
+def inverse_square(kk, kx, mask):
+    squared = kk + kx * kx
+    live = squared > 0.0
+    return jnp.where(live, mask / jnp.where(live, squared, 1.0), 0.0)
+
+
+def solve_fine(planes, kx, inverse, t):
     hat = [table_by(t, "f_z", stacked(p, turn_back(p))) for p in planes]
     kz = t["f_kz"][...]
     ky = jnp.broadcast_to(t["f_ky"][0:1, :], kz.shape)
-    squared = t["f_kk"][...] + kx * kx
-    live = squared > 0.0
-    inverse = jnp.where(live, t["f_mz"][...] * mx / jnp.where(live, squared, 1.0), 0.0)
     out = []
     for r in cross((kx, ky, kz), hat):
         r = r * inverse
@@ -312,12 +332,9 @@
     return table_by(t, "c_x", stacked(b, -turn_back_c(b)))
 
 
-def velocity_modes(hat, kx, mx, t):
+def velocity_modes(hat, kx, inverse, t):
     kz = t["c_kz"][...]
     ky = jnp.broadcast_to(t["c_ky"][0:1, :], kz.shape)
-    squared = t["c_kk"][...] + kx * kx
-    live = squared > 0.0
-    inverse = jnp.where(live, t["c_mz"][...] * mx / jnp.where(live, squared, 1.0), 0.0)
     return [-turn_back_c(r * inverse) for r in cross((kx, ky, kz), hat)]
 
 
@@ -333,7 +350,7 @@
 
 
 def prolong(pair, t):
-    wide = exact(exact(t["p_x"][...], pair), t["p_y"][...])
+    wide = exact(exact(t["p_x"][...], pair), jnp.concatenate([t["p_y0"][...], t["p_y1"][...]], axis=1))
     return wide[:, :N], wide[:, N:]
 
 
@@ -346,7 +363,7 @@
     fs=pltpu.VMEM((6, PARTS * FINE, N), f32),
     fr=pltpu.VMEM((6, PARTS * FINE, N), f32),
     cs=pltpu.VMEM((6, PARTS * COARSE, N), f32),
-    cr=pltpu.VMEM((6, PARTS * COARSE, N), f32),
+    cr=pltpu.VMEM((7, PARTS * COARSE, N), f32),
     fh_next=pltpu.VMEM((4, 3, 2, N, N), f32),
     fh_prev=pltpu.VMEM((4, 3, 2, N, N), f32),
     fh_low=pltpu.VMEM((4, 3, 2, N, N), f32),
@@ -356,30 +373,38 @@
     ch_low=pltpu.VMEM((5, 3, M, N), f32),
     ch_high=pltpu.VMEM((5, 3, M, N), f32),
     hand_v=pltpu.VMEM((3, M, N), f32),
-    hand_u=pltpu.VMEM((3, M, N), f32),
     hand_m=pltpu.VMEM((3, M, N), f32),
     send_v=pltpu.VMEM((3, M, N), f32),
-    send_u=pltpu.VMEM((3, M, N), f32),
     send_m=pltpu.VMEM((3, M, N), f32),
     co=pltpu.VMEM((14, 3, M, N), f32),
+    inv_f=pltpu.VMEM((2, N, N), f32),
+    inv_c=pltpu.VMEM((M, N), f32),
     f_ssem=pltpu.SemaphoreType.DMA((6,)),
     f_rsem=pltpu.SemaphoreType.DMA((6,)),
-    c_ssem=pltpu.SemaphoreType.DMA((6,)),
-    c_rsem=pltpu.SemaphoreType.DMA((6,)),
+    c_ssem=pltpu.SemaphoreType.DMA((7,)),
+    c_rsem=pltpu.SemaphoreType.DMA((7,)),
     h_ssem=pltpu.SemaphoreType.DMA((9, 2)),
     h_rsem=pltpu.SemaphoreType.DMA((9, 2)),
-    y_ssem=pltpu.SemaphoreType.DMA((4,)),
-    y_rsem=pltpu.SemaphoreType.DMA((4,)),
+    y_ssem=pltpu.SemaphoreType.DMA((3,)),
+    y_rsem=pltpu.SemaphoreType.DMA((3,)),
+    in_sem=pltpu.SemaphoreType.DMA((OPERANDS,)),
 )
 A0, A2, UA0, UA2, G0, G2, C1, C2, CM1, CM2, B1, S1, BM1, SM1 = range(14)
 
 
 def kernel(*refs):
-    count = len(NAMES)
-    init, end, old = refs[:3]
-    t = dict(zip(NAMES, refs[3 : 3 + count]))
-    nodes, q_out = refs[3 + count : 5 + count]
-    s = dict(zip(SCRATCH, refs[5 + count :]))
+    nodes, q_out = refs[OPERANDS : OPERANDS + 2]
+    staged = refs[OPERANDS + 2 : 2 * OPERANDS + 2]
+    init, end, old = staged[:3]
+    s = dict(zip(SCRATCH, refs[2 * OPERANDS + 2 :]))
+    t = {}
+    for places, packed in ((PLACES_32, staged[3]), (PLACES_16, staged[4])):
+        for name, (top, shape) in places.items():
+            t[name] = packed.at[pl.ds(top, shape[0]), pl.ds(0, shape[1])]
+    loads = [
+        pltpu.make_async_copy(source, target, s["in_sem"].at[i])
+        for i, (source, target) in enumerate(zip(refs[:OPERANDS], staged))
+    ]
     co = s["co"]
     row = lax.axis_index("tm")
     me = lax.axis_index("space")
@@ -394,39 +419,59 @@
         pl.semaphore_signal(barrier, inc=1, device_id=(row, lax.rem(me + k, PARTS)), device_id_type=MESH)
         return carry
 
+    def greet_rows(k, carry):
+        for other in (up, down):
+            pl.semaphore_signal(barrier, inc=1, device_id=(other, lax.rem(me + k, PARTS)), device_id_type=MESH)
+        return carry
+
+    for i in (0, 1, 4, 3, 2):
+        loads[i].start()
+    lax.fori_loop(0, PARTS, greet_rows, 0)
     lax.fori_loop(1, PARTS, greet, 0)
-    pl.semaphore_signal(barrier, inc=1, device_id=(up, me), device_id_type=MESH)
-    pl.semaphore_signal(barrier, inc=1, device_id=(down, me), device_id_type=MESH)
-    pl.semaphore_wait(barrier, PARTS + 1)
-
-
-    def transpose_start(send, recv, depth, ssem, rsem):
+    for i in (0, 1, 3, 4):
+        loads[i].wait()
+
+
+    place_x, place_z, core = me // 16, lax.rem(me // 2, 8), lax.rem(me, 2)
+
+    def transpose_start(send, recv, depth, ssem, rsem, to_row=None):
         mine = pl.ds(me * depth, depth)
-        pltpu.make_async_copy(send.at[mine], recv.at[mine], rsem).start()
-
-        def step(k, carry):
-            to = lax.rem(me + k, PARTS)
+
+        def post(z, x, c):
+            to = (lax.rem(place_x + x, 4) * 8 + lax.rem(place_z + z, 8)) * 2 + lax.rem(core + c, 2)
             pltpu.make_async_remote_copy(
                 src_ref=send.at[pl.ds(to * depth, depth)],
                 dst_ref=recv.at[mine],
                 send_sem=ssem,
                 recv_sem=rsem,
-                device_id=(row, to),
+                device_id=(row if to_row is None else to_row, to),
                 device_id_type=MESH,
             ).start()
+
+        def step(j, carry):
+            z = 4 + ((j + 1) // 2) * (1 - 2 * lax.rem(j, 2))
+            for x in (2, 1, 3, 0):
+                for c in (1, 0):
+                    post(z, x, c)
             return carry
 
-        lax.fori_loop(1, PARTS, step, 0)
+        lax.fori_loop(0, 7, step, 0)
+        for x in (2, 1, 3, 0):
+            for c in (1, 0):
+                if x or c or to_row is not None:
+                    post(0, x, c)
+        if to_row is None:
+            pltpu.make_async_copy(send.at[mine], recv.at[mine], rsem).start()
 
     def arrived(ref, sem):
         pltpu.make_async_copy(ref, ref, sem).wait()
 
-    def left(ref, depth, sem):
-        part = ref.at[pl.ds(0, (PARTS - 1) * depth)]
+    def left(ref, depth, sem, parts=PARTS - 1):
+        part = ref.at[pl.ds(0, parts * depth)]
         pltpu.make_async_copy(part, part, sem).wait()
 
-    def fine_start(i):
-        transpose_start(s["fs"].at[i], s["fr"].at[i], FINE, s["f_ssem"].at[i], s["f_rsem"].at[i])
+    def fine_start(i, to_row=None):
+        transpose_start(s["fs"].at[i], s["fr"].at[i], FINE, s["f_ssem"].at[i], s["f_rsem"].at[i], to_row)
 
     def coarse_start(i):
         transpose_start(s["cs"].at[i], s["cr"].at[i], COARSE, s["c_ssem"].at[i], s["c_rsem"].at[i])
@@ -481,8 +526,7 @@
 
     start_copy = hand_copy(end.at[0], s["node"].at[0], 0)
     v_copy = hand_copy(s["send_v"], s["hand_v"], 1)
-    u_copy = hand_copy(s["send_u"], s["hand_u"], 2)
-    m_copy = hand_copy(s["send_m"], s["hand_m"], 3)
+    m_copy = hand_copy(s["send_m"], s["hand_m"], 2)
     is_first = row == 0
     has_next = row < ROWS - 1
 
@@ -505,8 +549,7 @@
             ]
             at = pl.ds(me * 2 + low, 1)
             kx = jnp.broadcast_to(t["f_kx"][at, :], (N, N))
-            mx = jnp.broadcast_to(t["f_mx"][at, :], (N, N))
-            for c, out in enumerate(solve_fine(planes, kx, mx, t)):
+            for c, out in enumerate(solve_fine(planes, kx, s["inv_f"][low], t)):
                 for z in range(2):
                     s["fs"][i + 1, pl.ds((c * 2 + z) * 2 + low, PARTS, stride=FINE), :] = out[z * M : z * M + M]
 
@@ -580,12 +623,11 @@
     wide = lambda name: jnp.broadcast_to(t[name][mine, :], (M, N))
 
     def coarse_back(hat, i):
-        modes = velocity_modes(hat, wide("c_kx"), wide("c_mx"), t)
+        modes = velocity_modes(hat, wide("c_kx"), s["inv_c"][...], t)
         for c in range(3):
             s["cs"][i, pl.ds(c, PARTS, stride=COARSE), :] = z_coarse_back(modes[c], t)
 
-    def coarse_flux(u, w, i):
-        f = cross(u, w)
+    def coarse_halo(f, w, i):
         g = (-f[1], f[0], None)
         for c in range(3):
             nxt, prv = NU * c_second_next(w[c]), NU * c_second_prev(w[c])
@@ -594,7 +636,6 @@
             s["ch_next"][i, c] = nxt
             s["ch_prev"][i, c] = prv
         halo_start("c", i, 4 + i)
-        return f
 
     def coarse_tendency(f, w, i):
         own = [NU * (second_coarse_xy(w[c]) + c_second_own(w[c])) for c in range(3)]
@@ -616,45 +657,60 @@
     def restricted(get):
         return [restrict(get(c, 0), get(c, 1), t) for c in range(3)]
 
-
-    @pl.when(has_next)
-    def _():
-        start_copy.start()
-
-    @pl.when(is_first)
-    def _():
-        for c in range(3):
-            for z in range(2):
-                node[0, c, z] = init[c, z]
-
-    @pl.when(jnp.logical_not(is_first))
-    def _():
-        start_copy.wait_recv()
+    for low in range(2):
+        at = pl.ds(me * 2 + low, 1)
+        kx = jnp.broadcast_to(t["f_kx"][at, :], (N, N))
+        mask = t["f_mz"][...] * jnp.broadcast_to(t["f_mx"][at, :], (N, N))
+        s["inv_f"][low] = inverse_square(t["f_kk"][...], kx, mask)
+    s["inv_c"][...] = inverse_square(t["c_kk"][...], wide("c_kx"), t["c_mz"][...] * wide("c_mx"))
 
     f0 = lambda c, z: old[0, 0, c, z]
     f1 = lambda c, z: old[0, 1, c, z]
     f2 = lambda c, z: old[0, 2, c, z]
 
     for m in range(3):
-        fine_send(lambda c, z: node[m, c, z], 2 * m)
-        fine_start(2 * m)
         if m == 0:
-            keep(A0, restricted(lambda c, z: node[0, c, z]))
+            fine_send(lambda c, z: jnp.where(has_next, end[0, c, z], init[c, z]), 0)
+            pl.semaphore_wait(barrier, 3 * PARTS - 1)
+            fine_start(0, up)
+        else:
+            fine_send(lambda c, z: node[m, c, z], 2 * m)
+            fine_start(2 * m)
         if m == 1:
             keep(UA0, restricted(lambda c, z: speed[c, z]))
-            flux_g0 = coarse_flux(kept(UA0), kept(A0), 0)
+            flux_g0 = cross(kept(UA0), kept(A0))
+            coarse_halo(flux_g0, kept(A0), 0)
             keep(G0, coarse_tendency(flux_g0, kept(A0), 0))
         if m == 2:
             keep(A2, restricted(lambda c, z: node[2, c, z]))
         fine_wait(2 * m)
         fine_modes(2 * m)
         fine_start(2 * m + 1)
+        if m == 0:
+
+            @pl.when(has_next)
+            def _():
+                start_copy.start()
+
+            @pl.when(is_first)
+            def _():
+                for c in range(3):
+                    for z in range(2):
+                        node[0, c, z] = init[c, z]
+
+            @pl.when(jnp.logical_not(is_first))
+            def _():
+                start_copy.wait_recv()
+
+            keep(A0, restricted(lambda c, z: node[0, c, z]))
+            loads[2].wait()
         fine_wait(2 * m + 1)
         fine_velocity(2 * m + 1)
         fine_flux(m)
         if m == 2:
             keep(UA2, restricted(lambda c, z: speed[c, z]))
-            flux_g2 = coarse_flux(kept(UA2), kept(A2), 1)
+            flux_g2 = cross(kept(UA2), kept(A2))
+            coarse_halo(flux_g2, kept(A2), 1)
         weight = (DT / 6.0, DT * 2.0 / 3.0, DT / 6.0)[m]
         if m < 2:
             for c in range(3):
@@ -729,11 +785,12 @@
         coarse_wait(1)
         keep(CM2, coarse_modes(1))
         v_copy.wait_recv()
-        u_copy.wait_recv()
         start = [s["hand_v"][c] for c in range(3)]
-        f = coarse_flux([s["hand_u"][c] for c in range(3)], start, 2)
+        coarse_wait(6)
+        f = cross(coarse_velocity(6), start)
         coarse_send(f, 2)
         coarse_start(2)
+        coarse_halo(f, start, 2)
         early = coarse_tendency(f, start, 2)
         keep(B1, [start[c] + DT * early[c] + co[C1, c] for c in range(3)])
         keep(S1, [start[c] + HALF * early[c] + co[C2, c] for c in range(3)])
@@ -754,9 +811,10 @@
 
     coarse_wait(3)
     middle = kept(B1)
-    f = coarse_flux(coarse_velocity(3), middle, 3)
+    f = cross(coarse_velocity(3), middle)
     coarse_send(f, 4)
     coarse_start(4)
+    coarse_halo(f, middle, 3)
     later = coarse_tendency(f, middle, 3)
     for c in range(3):
         s["send_v"][c] = co[S1, c] + HALF * later[c]
@@ -770,11 +828,13 @@
     for c in range(3):
         s["send_m"][c] = co[SM1, c] + HALF * later[c]
     coarse_back([s["send_m"][c] for c in range(3)], 5)
-    coarse_start(5)
 
     @pl.when(has_next)
     def _():
+        transpose_start(s["cs"].at[5], s["cr"].at[6], COARSE, s["c_ssem"].at[6], s["c_rsem"].at[6], up)
         m_copy.start()
+
+    coarse_start(5)
 
     for c in range(3):
         zero = prolong(s["hand_v"][c] - co[A0, c], t)
@@ -793,12 +853,6 @@
 
     coarse_wait(5)
     out = coarse_velocity(5)
-    for c in range(3):
-        s["send_u"][c] = out[c]
-
-    @pl.when(has_next)
-    def _():
-        u_copy.start()
 
     change = [out[c] - co[UA2, c] for c in range(3)]
     for c in range(3):
@@ -824,7 +878,7 @@
         q_out[0, z] = -0.5 * diagonal - mixed
 
     for i in range(6):
-        left(s["fs"].at[i], FINE, s["f_ssem"].at[i])
+        left(s["fs"].at[i], FINE, s["f_ssem"].at[i], PARTS if i == 0 else PARTS - 1)
     for i in (0, 1, 3, 4, 5):
         left(s["cs"].at[i], COARSE, s["c_ssem"].at[i])
 
@@ -840,25 +894,27 @@
 
     @pl.when(has_next)
     def _():
-        for copy in (start_copy, v_copy, u_copy, m_copy):
+        left(s["cs"].at[5], COARSE, s["c_ssem"].at[6], PARTS)
+        for copy in (start_copy, v_copy, m_copy):
             copy.wait_send()
 
 
 def body(initial_state, end_states, old_tendencies):
     vmem = pl.BlockSpec(memory_space=pltpu.VMEM)
+    operands = [initial_state, end_states, old_tendencies, jnp.asarray(PACKED_32), jnp.asarray(PACKED_16)]
     return pl.pallas_call(
         kernel,
         out_shape=(
             jax.ShapeDtypeStruct((1, 3, 3, 2, N, N), f32),
             jax.ShapeDtypeStruct((1, 2, N, N), f32),
         ),
-        in_specs=[vmem] * (3 + len(NAMES)),
+        in_specs=[pl.BlockSpec(memory_space=pl.ANY)] * len(operands),
         out_specs=(vmem, vmem),
-        scratch_shapes=list(SCRATCH.values()),
+        scratch_shapes=[pltpu.VMEM(x.shape, x.dtype) for x in operands] + list(SCRATCH.values()),
         compiler_params=pltpu.CompilerParams(
             collective_id=0, has_side_effects=True, vmem_limit_bytes=56 * 1024 * 1024
         ),
-    )(initial_state, end_states, old_tendencies, *[jnp.asarray(TABLES[name]) for name in NAMES])
+    )(*operands)
 
 
 def solution(mesh):

time: 269 us -> 242 us (0.90)
  Pallas kernels: 265 us -> 238 us
    pallas_call x1, Pallas kernels: 265 us -> 238 us  [body(): pl.pallas_call(kernel, out_shape=(jax.ShapeDtypeStruct((1, 3, 3, 2, N, N)...]
where the time goes in v1:
time: 242 us
  Pallas kernels  238 us (98%)
  local copies, waits for them, and re-layouts  3.08 us (1%)
    pallas_call x1, Pallas kernels, body(): pl.pallas_call(kernel, out_shape=(jax.ShapeDtypeStruct((1, 3, 3, 2, N, N)...  238 us

profile of v1, /device:TPU:24, one launch (start us, length us, event | category | flops | bytes accessed | tf_op | source)
XLA Modules:
  0.0 242.1 jit_solution(5614161387284678514)
XLA Ops:
  0.6 238.3 %shard_map.68 = (f32[1,3,3,2,128,128]{5,4,3,2,1,0:T(8,128)}, f32[1,2,128,128]{3,2,1,0:T(8,128)}) custom-call(f32[3,2,128,128]{3,2,1,0:T(8,128)} %refs_0_.1, f32[1,3,2,128,128]{4,3,2,1,0:T(8,128)} %refs_1_.1, f32[1,3,3,2,128,128]{5,4,3,2,1,0:T(8,128)} %refs_2_.1, f32[2072,128]{1,0:T(8,128)} %constant.4.clone.refs_3_, bf16[2176,256]{1,0:T(8,128)(2,1)} %constant.5.clone.refs_4_), custom_call_target="tpu_custom_call" | custom-call | tf_op jit(solution)/shard_map/pallas_call | solution.py:905
  239.0 0.0 copy-start
  239.0 2.4 copy.9
  241.4 0.0 copy-done
  241.4 0.7 copy.10
Async XLA Ops:
  239.0 2.4 %copy-start = (f32[1,2,128,128]{3,2,1,0:T(8,128)S(1)}, f32[1,2,128,128]{3,2,1,0:T(8,128)}, u32[]{:S(2)}) copy-start(f32[1,2,128,128]{3,2,1,0:T(8,128)} %get-tuple-element.5) | copy-start | bytes 393220

commit v2 on v1

--- a/solution.py
+++ b/solution.py
@@ -15,7 +15,8 @@
 ROWS = 4
 N = 128
 M = 64
-FINE = 12
+FINE = 6
+THIRD = 4
 COARSE = 3
 f32 = jnp.float32
 MESH = pl.DeviceIdType.MESH
@@ -157,10 +158,10 @@
     return dot(high, table) + (dot(low, table) + dot(high, t[name + "_l"][...]))
 
 
-def table_by(t, name, x):
+def table_by(t, name, x, rows=slice(None)):
     high, low = split(x)
-    table = t[name + "_h"][...]
-    return dot(table, high) + (dot(table, low) + dot(t[name + "_l"][...], high))
+    table = t[name + "_h"][rows, :]
+    return dot(table, high) + (dot(table, low) + dot(t[name + "_l"][rows, :], high))
 
 
 def roll(x, shift, axis):
@@ -288,20 +289,9 @@
     return lane_pair(f, (-30 * T12, 16 * T12), (-30 * T12, 16 * T12))
 
 
-def forward_fine(plane, t):
-    return table_by(t, "f_x", both_halves(by_table(plane, t, "f_y")))
-
-
-def inverse_fine(modes, t):
-    return table_by(t, "i_x", both_halves(by_table(modes, t, "i_y")))
-
-
-def forward_coarse(pair, t):
-    return table_by(t, "c_x", both_halves(by_table(pair, t, "cf_y")))
-
-
-def inverse_coarse(modes, t):
-    return table_by(t, "c_x", both_halves(by_table(modes, t, "ci_y")))
+def along_both(fields, t, name):
+    wide = by_table(jnp.concatenate(fields, axis=0), t, name)
+    return [table_by(t, "c_x", both_halves(wide[c * M : c * M + M])) for c in range(len(fields))]
 
 
 def inverse_square(kk, kx, mask):
@@ -360,6 +350,9 @@
     flux=pltpu.VMEM((3, 2, N, N), f32),
     total=pltpu.VMEM((3, 2, N, N), f32),
     slope=pltpu.VMEM((3, 2, N, N), f32),
+    half=pltpu.VMEM((3, 2, 2 * N, N), f32),
+    gs=pltpu.VMEM((9, PARTS * THIRD, N), f32),
+    gr=pltpu.VMEM((9, PARTS * THIRD, N), f32),
     fs=pltpu.VMEM((6, PARTS * FINE, N), f32),
     fr=pltpu.VMEM((6, PARTS * FINE, N), f32),
     cs=pltpu.VMEM((6, PARTS * COARSE, N), f32),
@@ -379,12 +372,14 @@
     co=pltpu.VMEM((14, 3, M, N), f32),
     inv_f=pltpu.VMEM((2, N, N), f32),
     inv_c=pltpu.VMEM((M, N), f32),
+    g_ssem=pltpu.SemaphoreType.DMA((9,)),
+    g_rsem=pltpu.SemaphoreType.DMA((9,)),
     f_ssem=pltpu.SemaphoreType.DMA((6,)),
     f_rsem=pltpu.SemaphoreType.DMA((6,)),
     c_ssem=pltpu.SemaphoreType.DMA((7,)),
     c_rsem=pltpu.SemaphoreType.DMA((7,)),
-    h_ssem=pltpu.SemaphoreType.DMA((9, 2)),
-    h_rsem=pltpu.SemaphoreType.DMA((9, 2)),
+    h_ssem=pltpu.SemaphoreType.DMA((17, 2)),
+    h_rsem=pltpu.SemaphoreType.DMA((17, 2)),
     y_ssem=pltpu.SemaphoreType.DMA((3,)),
     y_rsem=pltpu.SemaphoreType.DMA((3,)),
     in_sem=pltpu.SemaphoreType.DMA((OPERANDS,)),
@@ -415,30 +410,37 @@
 
     barrier = pltpu.get_barrier_semaphore()
 
-    def greet(k, carry):
-        pl.semaphore_signal(barrier, inc=1, device_id=(row, lax.rem(me + k, PARTS)), device_id_type=MESH)
-        return carry
-
-    def greet_rows(k, carry):
-        for other in (up, down):
-            pl.semaphore_signal(barrier, inc=1, device_id=(other, lax.rem(me + k, PARTS)), device_id_type=MESH)
+    place_x, place_z, core = me // 16, lax.rem(me // 2, 8), lax.rem(me, 2)
+
+    def partner(z, x, c):
+        return (lax.rem(place_x + x, 4) * 8 + lax.rem(place_z + z, 8)) * 2 + lax.rem(core + c, 2)
+
+    def greet(z, x, c, rows):
+        for other in rows:
+            pl.semaphore_signal(barrier, inc=1, device_id=(other, partner(z, x, c)), device_id_type=MESH)
+
+    def greet_far(j, carry):
+        z = 4 + ((j + 1) // 2) * (1 - 2 * lax.rem(j, 2))
+        for x in (2, 1, 3, 0):
+            for c in (1, 0):
+                greet(z, x, c, (up, down, row))
         return carry
 
     for i in (0, 1, 4, 3, 2):
         loads[i].start()
-    lax.fori_loop(0, PARTS, greet_rows, 0)
-    lax.fori_loop(1, PARTS, greet, 0)
+    lax.fori_loop(0, 7, greet_far, 0)
+    for x in (2, 1, 3, 0):
+        for c in (1, 0):
+            greet(0, x, c, (up, down, row) if x or c else (up, down))
     for i in (0, 1, 3, 4):
         loads[i].wait()
 
 
-    place_x, place_z, core = me // 16, lax.rem(me // 2, 8), lax.rem(me, 2)
-
     def transpose_start(send, recv, depth, ssem, rsem, to_row=None):
         mine = pl.ds(me * depth, depth)
 
         def post(z, x, c):
-            to = (lax.rem(place_x + x, 4) * 8 + lax.rem(place_z + z, 8)) * 2 + lax.rem(core + c, 2)
+            to = partner(z, x, c)
             pltpu.make_async_remote_copy(
                 src_ref=send.at[pl.ds(to * depth, depth)],
                 dst_ref=recv.at[mine],
@@ -470,8 +472,14 @@
         part = ref.at[pl.ds(0, parts * depth)]
         pltpu.make_async_copy(part, part, sem).wait()
 
-    def fine_start(i, to_row=None):
-        transpose_start(s["fs"].at[i], s["fr"].at[i], FINE, s["f_ssem"].at[i], s["f_rsem"].at[i], to_row)
+    def third_start(i, to_row):
+        transpose_start(s["gs"].at[i], s["gr"].at[i], THIRD, s["g_ssem"].at[i], s["g_rsem"].at[i], to_row)
+
+    def third_wait(i):
+        arrived(s["gr"].at[i], s["g_rsem"].at[i])
+
+    def fine_start(i):
+        transpose_start(s["fs"].at[i], s["fr"].at[i], FINE, s["f_ssem"].at[i], s["f_rsem"].at[i])
 
     def coarse_start(i):
         transpose_start(s["cs"].at[i], s["cr"].at[i], COARSE, s["c_ssem"].at[i], s["c_rsem"].at[i])
@@ -482,36 +490,35 @@
     def coarse_wait(i):
         arrived(s["cr"].at[i], s["c_rsem"].at[i])
 
-    def halo_copies(kind, i, sem):
-        return (
-            pltpu.make_async_remote_copy(
-                src_ref=s[kind + "h_next"].at[i],
-                dst_ref=s[kind + "h_low"].at[i],
-                send_sem=s["h_ssem"].at[sem, 0],
-                recv_sem=s["h_rsem"].at[sem, 0],
-                device_id=(row, ahead),
+    def halo_copies(kind, at, sem):
+        def copy(out, into, side, to):
+            return pltpu.make_async_remote_copy(
+                src_ref=s[kind + out].at[at],
+                dst_ref=s[kind + into].at[at],
+                send_sem=s["h_ssem"].at[sem, side],
+                recv_sem=s["h_rsem"].at[sem, side],
+                device_id=(row, to),
                 device_id_type=MESH,
-            ),
-            pltpu.make_async_remote_copy(
-                src_ref=s[kind + "h_prev"].at[i],
-                dst_ref=s[kind + "h_high"].at[i],
-                send_sem=s["h_ssem"].at[sem, 1],
-                recv_sem=s["h_rsem"].at[sem, 1],
-                device_id=(row, behind),
-                device_id_type=MESH,
-            ),
-        )
-
-    def halo_start(kind, i, sem):
-        for copy in halo_copies(kind, i, sem):
+            )
+
+        return copy("h_next", "h_low", 0, ahead), copy("h_prev", "h_high", 1, behind)
+
+    def fine_halo(m, c):
+        return halo_copies("f", (m, c), 3 * m + c)
+
+    def coarse_halo_copies(i):
+        return halo_copies("c", i, 12 + i)
+
+    def begin(copies):
+        for copy in copies:
             copy.start()
 
-    def halo_wait(kind, i, sem):
-        for copy in halo_copies(kind, i, sem):
+    def landed(copies):
+        for copy in copies:
             copy.wait_recv()
 
-    def halo_left(kind, i, sem):
-        for copy in halo_copies(kind, i, sem):
+    def gone(copies):
+        for copy in copies:
             copy.wait_send()
 
     def hand_copy(src, dst, sem):
@@ -531,37 +538,54 @@
     has_next = row < ROWS - 1
 
 
-    def fine_send(get, i):
+    def fine_spread(c, z, plane):
+        s["half"][c, z] = both_halves(by_table(plane, t, "f_y"))
+
+
+    def send_z(m, to_row=None):
+        for z in range(2):
+            out = table_by(t, "f_x", s["half"][2, z])
+            for low in range(2):
+                s["gs"][3 * m, pl.ds(2 * low + z, PARTS, stride=THIRD), :] = out[low * M : low * M + M]
+        third_start(3 * m, to_row)
+
+    def send_xy(m, to_row=None):
+        for low in range(2):
+            for c in range(2):
+                for z in range(2):
+                    s["gs"][3 * m + 1 + low, pl.ds(2 * c + z, PARTS, stride=THIRD), :] = table_by(
+                        t, "f_x", s["half"][c, z], slice(low * M, low * M + M)
+                    )
+            third_start(3 * m + 1 + low, to_row)
+
+    def fine_modes(m):
+        third_wait(3 * m)
+        for low in range(2):
+            third_wait(3 * m + 1 + low)
+            places = [(1 + low, 0), (1 + low, 2), (0, 2 * low)]
+            planes = [
+                stacked(*[s["gr"][3 * m + part, pl.ds(at + z, PARTS, stride=THIRD), :] for z in range(2)])
+                for part, at in places
+            ]
+            kx = jnp.broadcast_to(t["f_kx"][pl.ds(me * 2 + low, 1), :], (N, N))
+            for c, out in enumerate(solve_fine(planes, kx, s["inv_f"][low], t)):
+                for z in range(2):
+                    s["fs"][2 * m + low, pl.ds(c * 2 + z, PARTS, stride=FINE), :] = out[z * M : z * M + M]
+            fine_start(2 * m + low)
+
+    def fine_velocity(m):
+        for low in range(2):
+            fine_wait(2 * m + low)
+            for c in range(3):
+                modes = stacked(*[s["fr"][2 * m + low, pl.ds(c * 2 + z, PARTS, stride=FINE), :] for z in range(2)])
+                wide = by_table(modes, t, "i_y")
+                for z in range(2):
+                    part = wide[z * M : z * M + M]
+                    s["half"][c, z, low * M : low * M + M, :] = part[:, :N]
+                    s["half"][c, z, N + low * M : N + low * M + M, :] = part[:, N:]
         for c in range(3):
             for z in range(2):
-                out = forward_fine(get(c, z), t)
-                for low in range(2):
-                    s["fs"][i, pl.ds((c * 2 + z) * 2 + low, PARTS, stride=FINE), :] = out[low * M : low * M + M]
-
-    def fine_modes(i):
-        for low in range(2):
-            planes = [
-                stacked(
-                    s["fr"][i, pl.ds((c * 2) * 2 + low, PARTS, stride=FINE), :],
-                    s["fr"][i, pl.ds((c * 2 + 1) * 2 + low, PARTS, stride=FINE), :],
-                )
-                for c in range(3)
-            ]
-            at = pl.ds(me * 2 + low, 1)
-            kx = jnp.broadcast_to(t["f_kx"][at, :], (N, N))
-            for c, out in enumerate(solve_fine(planes, kx, s["inv_f"][low], t)):
-                for z in range(2):
-                    s["fs"][i + 1, pl.ds((c * 2 + z) * 2 + low, PARTS, stride=FINE), :] = out[z * M : z * M + M]
-
-    def fine_velocity(i):
-        for c in range(3):
-            for z in range(2):
-                at = (c * 2 + z) * 2
-                modes = stacked(
-                    s["fr"][i, pl.ds(at, PARTS, stride=FINE), :],
-                    s["fr"][i, pl.ds(at + 1, PARTS, stride=FINE), :],
-                )
-                s["speed"][c, z] = inverse_fine(modes, t)
+                s["speed"][c, z] = table_by(t, "i_x", s["half"][c, z])
 
     node, speed, flux, total = s["node"], s["speed"], s["flux"], s["total"]
 
@@ -570,22 +594,25 @@
             parts = cross([speed[c, z] for c in range(3)], [node[m, c, z] for c in range(3)])
             for c in range(3):
                 flux[c, z] = parts[c]
-        for c in range(3):
-            w0, w1 = node[m, c, 0], node[m, c, 1]
-            ahead0, ahead1 = second_next(w0, w1)
-            back0, back1 = second_prev(w0, w1)
-            ahead0, ahead1, back0, back1 = NU * ahead0, NU * ahead1, NU * back0, NU * back1
-            if c < 2:
-                sign = -1.0 if c == 0 else 1.0
-                g0, g1 = sign * flux[1 - c, 0], sign * flux[1 - c, 1]
-                d0, d1 = first_next(g0, g1)
-                e0, e1 = first_prev(g0, g1)
-                ahead0, ahead1, back0, back1 = ahead0 + d0, ahead1 + d1, back0 + e0, back1 + e1
-            s["fh_next"][m, c, 0] = ahead0
-            s["fh_next"][m, c, 1] = ahead1
-            s["fh_prev"][m, c, 0] = back0
-            s["fh_prev"][m, c, 1] = back1
-        halo_start("f", m, m)
+        for c in range(2):
+            fine_shares(m, c)
+
+    def fine_shares(m, c):
+        w0, w1 = node[m, c, 0], node[m, c, 1]
+        ahead0, ahead1 = second_next(w0, w1)
+        back0, back1 = second_prev(w0, w1)
+        ahead0, ahead1, back0, back1 = NU * ahead0, NU * ahead1, NU * back0, NU * back1
+        if c < 2:
+            sign = -1.0 if c == 0 else 1.0
+            g0, g1 = sign * flux[1 - c, 0], sign * flux[1 - c, 1]
+            d0, d1 = first_next(g0, g1)
+            e0, e1 = first_prev(g0, g1)
+            ahead0, ahead1, back0, back1 = ahead0 + d0, ahead1 + d1, back0 + e0, back1 + e1
+        s["fh_next"][m, c, 0] = ahead0
+        s["fh_next"][m, c, 1] = ahead1
+        s["fh_prev"][m, c, 0] = back0
+        s["fh_prev"][m, c, 1] = back1
+        begin(fine_halo(m, c))
 
     def fine_local(m, c):
         w0, w1 = node[m, c, 0], node[m, c, 1]
@@ -607,8 +634,8 @@
 
 
     def coarse_send(values, i):
-        for c in range(3):
-            s["cs"][i, pl.ds(c, PARTS, stride=COARSE), :] = forward_coarse(values[c], t)
+        for c, out in enumerate(along_both(values, t, "cf_y")):
+            s["cs"][i, pl.ds(c, PARTS, stride=COARSE), :] = out
 
     def coarse_recv(i):
         return [s["cr"][i, pl.ds(c, PARTS, stride=COARSE), :] for c in range(3)]
@@ -617,7 +644,7 @@
         return [z_coarse(x, t) for x in coarse_recv(i)]
 
     def coarse_velocity(i):
-        return [inverse_coarse(x, t) for x in coarse_recv(i)]
+        return along_both(coarse_recv(i), t, "ci_y")
 
     mine = pl.ds(me, 1)
     wide = lambda name: jnp.broadcast_to(t[name][mine, :], (M, N))
@@ -635,7 +662,7 @@
                 nxt, prv = nxt + c_first_next(g[c]), prv + c_first_prev(g[c])
             s["ch_next"][i, c] = nxt
             s["ch_prev"][i, c] = prv
-        halo_start("c", i, 4 + i)
+        begin(coarse_halo_copies(i))
 
     def coarse_tendency(f, w, i):
         own = [NU * (second_coarse_xy(w[c]) + c_second_own(w[c])) for c in range(3)]
@@ -644,7 +671,7 @@
             c_first_own(f[0]) - first_coarse(f[2], True),
             first_coarse(f[1], True) - first_coarse(f[0], False),
         ]
-        halo_wait("c", i, 4 + i)
+        landed(coarse_halo_copies(i))
         return [own[c] + parts[c] + (s["ch_low"][i, c] + s["ch_high"][i, c]) for c in range(3)]
 
     def keep(i, values):
@@ -668,14 +695,18 @@
     f1 = lambda c, z: old[0, 1, c, z]
     f2 = lambda c, z: old[0, 2, c, z]
 
+    for c in range(3):
+        for z in range(2):
+            fine_spread(c, z, jnp.where(has_next, end[0, c, z], init[c, z]))
+    pl.semaphore_wait(barrier, 3 * PARTS - 1)
+
     for m in range(3):
         if m == 0:
-            fine_send(lambda c, z: jnp.where(has_next, end[0, c, z], init[c, z]), 0)
-            pl.semaphore_wait(barrier, 3 * PARTS - 1)
-            fine_start(0, up)
+            send_z(0, up)
+            send_xy(0, up)
         else:
-            fine_send(lambda c, z: node[m, c, z], 2 * m)
-            fine_start(2 * m)
+            send_xy(m)
+            fine_shares(m, 2)
         if m == 1:
             keep(UA0, restricted(lambda c, z: speed[c, z]))
             flux_g0 = cross(kept(UA0), kept(A0))
@@ -683,9 +714,7 @@
             keep(G0, coarse_tendency(flux_g0, kept(A0), 0))
         if m == 2:
             keep(A2, restricted(lambda c, z: node[2, c, z]))
-        fine_wait(2 * m)
-        fine_modes(2 * m)
-        fine_start(2 * m + 1)
+        fine_modes(m)
         if m == 0:
 
             @pl.when(has_next)
@@ -702,10 +731,10 @@
             def _():
                 start_copy.wait_recv()
 
+            fine_shares(0, 2)
             keep(A0, restricted(lambda c, z: node[0, c, z]))
             loads[2].wait()
-        fine_wait(2 * m + 1)
-        fine_velocity(2 * m + 1)
+        fine_velocity(m)
         fine_flux(m)
         if m == 2:
             keep(UA2, restricted(lambda c, z: speed[c, z]))
@@ -713,7 +742,7 @@
             coarse_halo(flux_g2, kept(A2), 1)
         weight = (DT / 6.0, DT * 2.0 / 3.0, DT / 6.0)[m]
         if m < 2:
-            for c in range(3):
+            def advance(c):
                 local = fine_local(m, c)
                 for z in range(2):
                     total[c, z] = weight * local[z] if m == 0 else total[c, z] + weight * local[z]
@@ -730,19 +759,30 @@
                             + (DT * 5.0 / 24.0) * f2(c, z)
                         )
                     node[m + 1, c, z] = node[m, c, z] + HALF * local[z] + old_part
-            halo_wait("f", m, m)
-            for c in range(3):
+
+            def finish(c):
+                landed(fine_halo(m, c))
                 for z in range(2):
                     share = s["fh_low"][m, c, z] + s["fh_high"][m, c, z]
                     total[c, z] = total[c, z] + weight * share
-                    node[m + 1, c, z] = node[m + 1, c, z] + HALF * share
+                    fresh = node[m + 1, c, z] + HALF * share
+                    node[m + 1, c, z] = fresh
+                    fine_spread(c, z, fresh)
+
+            advance(2)
+            finish(2)
+            send_z(m + 1)
+            for c in range(2):
+                advance(c)
+            for c in range(2):
+                finish(c)
         else:
             for c in range(3):
                 local = fine_local(m, c)
                 for z in range(2):
                     total[c, z] = total[c, z] + weight * local[z]
-            halo_wait("f", m, m)
-            for c in range(3):
+            for c in (2, 0, 1):
+                landed(fine_halo(m, c))
                 for z in range(2):
                     share = s["fh_low"][m, c, z] + s["fh_high"][m, c, z]
                     total[c, z] = total[c, z] + weight * share
@@ -762,15 +802,16 @@
     coarse_send(kept(C2), 1)
     coarse_start(1)
 
-    for c in range(3):
-        a, b = speed[c, 0], speed[c, 1]
-        s["fh_next"][3, c, 0], s["fh_next"][3, c, 1] = first_next(a, b)
-        s["fh_prev"][3, c, 0], s["fh_prev"][3, c, 1] = first_prev(a, b)
-    halo_start("f", 3, 3)
-
     coarse_wait(0)
     keep(CM1, coarse_modes(0))
     sx, lx = wide("c_sx"), wide("c_lx")
+
+    def end_shares():
+        for c in range(3):
+            a, b = speed[c, 0], speed[c, 1]
+            s["fh_next"][3, c, 0], s["fh_next"][3, c, 1] = first_next(a, b)
+            s["fh_prev"][3, c, 0], s["fh_prev"][3, c, 1] = first_prev(a, b)
+            begin(fine_halo(3, c))
 
     @pl.when(is_first)
     def _():
@@ -784,6 +825,7 @@
     def _():
         coarse_wait(1)
         keep(CM2, coarse_modes(1))
+        end_shares()
         v_copy.wait_recv()
         start = [s["hand_v"][c] for c in range(3)]
         coarse_wait(6)
@@ -834,7 +876,13 @@
         transpose_start(s["cs"].at[5], s["cr"].at[6], COARSE, s["c_ssem"].at[6], s["c_rsem"].at[6], up)
         m_copy.start()
 
-    coarse_start(5)
+    @pl.when(jnp.logical_not(has_next))
+    def _():
+        coarse_start(5)
+
+    @pl.when(is_first)
+    def _():
+        end_shares()
 
     for c in range(3):
         zero = prolong(s["hand_v"][c] - co[A0, c], t)
@@ -844,9 +892,13 @@
             nodes[0, 1, c, z] = node[1, c, z] + 0.5 * (zero[z] + two[z])
             nodes[0, 2, c, z] = node[2, c, z] + two[z]
 
-    halo_wait("f", 3, 3)
+    @pl.when(has_next)
+    def _():
+        coarse_start(5)
+
     slope = s["slope"]
     for c in range(3):
+        landed(fine_halo(3, c))
         own = first_own(speed[c, 0], speed[c, 1])
         for z in range(2):
             slope[c, z] = own[z] + (s["fh_low"][3, c, z] + s["fh_high"][3, c, z])
@@ -858,13 +910,13 @@
     for c in range(3):
         s["ch_next"][4, c] = c_first_next(change[c])
         s["ch_prev"][4, c] = c_first_prev(change[c])
-    halo_start("c", 4, 8)
+    begin(coarse_halo_copies(4))
     for c in range(3):
         put = prolong(change[c], t)
         for z in range(2):
             speed[c, z] = speed[c, z] + put[z]
     own = [c_first_own(change[c]) for c in range(3)]
-    halo_wait("c", 4, 8)
+    landed(coarse_halo_copies(4))
     for c in range(3):
         put = prolong(own[c] + (s["ch_low"][4, c] + s["ch_high"][4, c]), t)
         for z in range(2):
@@ -877,20 +929,23 @@
         mixed = gx[1] * gy[0] + gx[2] * gz[0] + gy[2] * gz[1]
         q_out[0, z] = -0.5 * diagonal - mixed
 
+    for i in range(9):
+        left(s["gs"].at[i], THIRD, s["g_ssem"].at[i], PARTS if i < 3 else PARTS - 1)
     for i in range(6):
-        left(s["fs"].at[i], FINE, s["f_ssem"].at[i], PARTS if i == 0 else PARTS - 1)
+        left(s["fs"].at[i], FINE, s["f_ssem"].at[i])
     for i in (0, 1, 3, 4, 5):
         left(s["cs"].at[i], COARSE, s["c_ssem"].at[i])
 
     @pl.when(jnp.logical_not(is_first))
     def _():
         left(s["cs"].at[2], COARSE, s["c_ssem"].at[2])
-        halo_left("c", 2, 6)
+        gone(coarse_halo_copies(2))
 
     for i in range(4):
-        halo_left("f", i, i)
+        for c in range(3):
+            gone(fine_halo(i, c))
     for i in (0, 1, 3, 4):
-        halo_left("c", i, 4 + i)
+        gone(coarse_halo_copies(i))
 
     @pl.when(has_next)
     def _():

time: 242 us -> 228 us (0.942)
  Pallas kernels: 238 us -> 224 us
    pallas_call x1, Pallas kernels: 238 us -> 224 us  [body(): pl.pallas_call(kernel, out_shape=(jax.ShapeDtypeStruct((1, 3, 3, 2, N, N)...]
where the time goes in v2:
time: 228 us
  Pallas kernels  224 us (98%)
  local copies, waits for them, and re-layouts  3.08 us (1%)
    pallas_call x1, Pallas kernels, body(): pl.pallas_call(kernel, out_shape=(jax.ShapeDtypeStruct((1, 3, 3, 2, N, N)...  224 us

profile of v2, /device:TPU:24, one launch (start us, length us, event | category | flops | bytes accessed | tf_op | source)
XLA Modules:
  0.0 227.5 jit_solution(12954077486061424298)
XLA Ops:
  0.6 223.8 %shard_map.68 = (f32[1,3,3,2,128,128]{5,4,3,2,1,0:T(8,128)}, f32[1,2,128,128]{3,2,1,0:T(8,128)}) custom-call(f32[3,2,128,128]{3,2,1,0:T(8,128)} %refs_0_.1, f32[1,3,2,128,128]{4,3,2,1,0:T(8,128)} %refs_1_.1, f32[1,3,3,2,128,128]{5,4,3,2,1,0:T(8,128)} %refs_2_.1, f32[2072,128]{1,0:T(8,128)} %constant.4.clone.refs_3_, bf16[2176,256]{1,0:T(8,128)(2,1)} %constant.5.clone.refs_4_), custom_call_target="tpu_custom_call" | custom-call | tf_op jit(solution)/shard_map/pallas_call | solution.py:960
  224.4 0.0 copy-start
  224.4 2.4 %copy.9 = f32[1,3,3,2,128,128]{5,4,3,2,1,0:T(8,128)} copy(f32[1,3,3,2,128,128]{5,4,3,2,1,0:T(8,128)} %get-tuple-element.4) | data formatting | bytes 2359296
  226.8 0.0 copy-done
  226.8 0.7 copy.10
Async XLA Ops:
  224.4 2.4 %copy-start = (f32[1,2,128,128]{3,2,1,0:T(8,128)S(1)}, f32[1,2,128,128]{3,2,1,0:T(8,128)}, u32[]{:S(2)}) copy-start(f32[1,2,128,128]{3,2,1,0:T(8,128)} %get-tuple-element.5) | copy-start | bytes 393220

commit v3 on v2

--- a/solution.py
+++ b/solution.py
@@ -75,7 +75,7 @@
     t["r_x"] = table
     t["r_y"] = twice(table.T)
     t["p_x"] = 4.0 * table.T
-    t["p_y0"], t["p_y1"] = np.hsplit(twice(table), 2)
+    t["p_y"] = twice(table)
     kx, _, _ = wave_symbols(signed(grid, N), N, 1.0)
     ky = np.tile(kx[:M], 2)[None, :]
     ones = np.ones((1, N))
@@ -111,13 +111,20 @@
         if name in SPLIT:
             high = value.astype(jnp.bfloat16)
             made[name + "_h"] = high
-            made[name + "_l"] = (value - high.astype(np.float32)).astype(jnp.bfloat16)
+            if name in RIGHT:
+                made[name + "_h"] = np.vstack([high, high])
+            if name in LEFT:
+                made[name + "_h"] = np.hstack([high, high])
+            low = (value - high.astype(np.float32)).astype(jnp.bfloat16)
+            made[name + "_l"] = np.hstack([low, np.zeros_like(low)]) if name in LEFT else low
         else:
             made[name] = value
     return made
 
 
-SPLIT = ("f_x", "f_y", "f_z", "i_x", "i_y", "i_z", "cf_y", "c_x", "ci_y")
+RIGHT = ("f_y", "i_y", "cf_y", "ci_y", "p_y")
+LEFT = ("c_x", "r_x", "p_x")
+SPLIT = ("r_x", "r_y", "p_x", "p_y", "f_x", "f_y", "f_z", "i_x", "i_y", "i_z", "cf_y", "c_x", "ci_y")
 TABLES = build_tables()
 
 
@@ -139,10 +146,6 @@
 OPERANDS = 5
 
 
-def exact(a, b):
-    return jnp.dot(a, b, precision=lax.Precision.HIGHEST, preferred_element_type=f32)
-
-
 def dot(a, b):
     return jnp.dot(a, b, preferred_element_type=f32)
 
@@ -155,12 +158,18 @@
 def by_table(x, t, name):
     high, low = split(x)
     table = t[name + "_h"][...]
-    return dot(high, table) + (dot(low, table) + dot(high, t[name + "_l"][...]))
+    rest = dot(high, t[name + "_l"][...])
+    if name in RIGHT:
+        return dot(jnp.concatenate([high, low], axis=1), table) + rest
+    return dot(high, table) + (dot(low, table) + rest)
 
 
 def table_by(t, name, x, rows=slice(None)):
     high, low = split(x)
     table = t[name + "_h"][rows, :]
+    if name in LEFT:
+        both = jnp.concatenate([high, low], axis=0)
+        return dot(table, both) + dot(t[name + "_l"][...], both)
     return dot(table, high) + (dot(table, low) + dot(t[name + "_l"][rows, :], high))
 
 
@@ -335,13 +344,14 @@
     return [-turn_back_c(r) + spread * w[i] for i, r in enumerate(cross((sx, sy, sz), flux))]
 
 
-def restrict(a, b, t):
-    return exact(t["r_x"][...], exact(jnp.concatenate([a, b], axis=1), t["r_y"][...]))
-
-
-def prolong(pair, t):
-    wide = exact(exact(t["p_x"][...], pair), jnp.concatenate([t["p_y0"][...], t["p_y1"][...]], axis=1))
-    return wide[:, :N], wide[:, N:]
+def restrict(pairs, t):
+    wide = by_table(jnp.concatenate([jnp.concatenate(pair, axis=1) for pair in pairs], axis=0), t, "r_y")
+    return [table_by(t, "r_x", wide[c * N : c * N + N]) for c in range(len(pairs))]
+
+
+def prolong(pairs, t):
+    wide = by_table(jnp.concatenate([table_by(t, "p_x", pair) for pair in pairs], axis=0), t, "p_y")
+    return [(wide[c * N : c * N + N, :N], wide[c * N : c * N + N, N:]) for c in range(len(pairs))]
 
 
 SCRATCH = dict(
@@ -361,6 +371,8 @@
     fh_prev=pltpu.VMEM((4, 3, 2, N, N), f32),
     fh_low=pltpu.VMEM((4, 3, 2, N, N), f32),
     fh_high=pltpu.VMEM((4, 3, 2, N, N), f32),
+    es=pltpu.VMEM((PARTS * 2 * COARSE, N), f32),
+    er=pltpu.VMEM((PARTS * 2 * COARSE, N), f32),
     ch_next=pltpu.VMEM((5, 3, M, N), f32),
     ch_prev=pltpu.VMEM((5, 3, M, N), f32),
     ch_low=pltpu.VMEM((5, 3, M, N), f32),
@@ -594,8 +606,9 @@
             parts = cross([speed[c, z] for c in range(3)], [node[m, c, z] for c in range(3)])
             for c in range(3):
                 flux[c, z] = parts[c]
-        for c in range(2):
-            fine_shares(m, c)
+        if m < 2:
+            for c in range(2):
+                fine_shares(m, c)
 
     def fine_shares(m, c):
         w0, w1 = node[m, c, 0], node[m, c, 1]
@@ -682,7 +695,7 @@
         return [co[i, c] for c in range(3)]
 
     def restricted(get):
-        return [restrict(get(c, 0), get(c, 1), t) for c in range(3)]
+        return restrict([(get(c, 0), get(c, 1)) for c in range(3)], t)
 
     for low in range(2):
         at = pl.ds(me * 2 + low, 1)
@@ -706,7 +719,8 @@
             send_xy(0, up)
         else:
             send_xy(m)
-            fine_shares(m, 2)
+            if m == 1:
+                fine_shares(m, 2)
         if m == 1:
             keep(UA0, restricted(lambda c, z: speed[c, z]))
             flux_g0 = cross(kept(UA0), kept(A0))
@@ -737,6 +751,8 @@
         fine_velocity(m)
         fine_flux(m)
         if m == 2:
+            small = restrict([(flux[c, 0], flux[c, 1]) for c in range(2)], t)
+            coarse_halo([*small, None], kept(A2), 4)
             keep(UA2, restricted(lambda c, z: speed[c, z]))
             flux_g2 = cross(kept(UA2), kept(A2))
             coarse_halo(flux_g2, kept(A2), 1)
@@ -781,13 +797,10 @@
                 local = fine_local(m, c)
                 for z in range(2):
                     total[c, z] = total[c, z] + weight * local[z]
-            for c in (2, 0, 1):
-                landed(fine_halo(m, c))
-                for z in range(2):
-                    share = s["fh_low"][m, c, z] + s["fh_high"][m, c, z]
-                    total[c, z] = total[c, z] + weight * share
 
     rest = restricted(lambda c, z: total[c, z])
+    landed(coarse_halo_copies(4))
+    rest = [rest[c] + (DT / 6.0) * (s["ch_low"][4, c] + s["ch_high"][4, c]) for c in range(3)]
     keep(C1, [rest[c] + jnp.where(is_first, co[A0, c], -DT * co[G0, c]) for c in range(3)])
     coarse_send(kept(C1), 0)
     coarse_start(0)
@@ -869,24 +882,35 @@
     later = tendency_modes(coarse_modes(4), kept(BM1), sx, lx, t)
     for c in range(3):
         s["send_m"][c] = co[SM1, c] + HALF * later[c]
-    coarse_back([s["send_m"][c] for c in range(3)], 5)
+    final = velocity_modes([s["send_m"][c] for c in range(3)], wide("c_kx"), s["inv_c"][...], t)
+    back = [z_coarse_back(x, t) for x in final]
 
     @pl.when(has_next)
     def _():
+        for c in range(3):
+            s["cs"][5, pl.ds(c, PARTS, stride=COARSE), :] = back[c]
         transpose_start(s["cs"].at[5], s["cr"].at[6], COARSE, s["c_ssem"].at[6], s["c_rsem"].at[6], up)
         m_copy.start()
 
+    back = back + [z_coarse_back(-turn_back_c(t["c_sz"][...] * x), t) for x in final]
+    for c in range(6):
+        s["es"][pl.ds(c, PARTS, stride=2 * COARSE), :] = back[c]
+
+    def end_start():
+        transpose_start(s["es"], s["er"], 2 * COARSE, s["c_ssem"].at[5], s["c_rsem"].at[5])
+
     @pl.when(jnp.logical_not(has_next))
     def _():
-        coarse_start(5)
+        end_start()
 
     @pl.when(is_first)
     def _():
         end_shares()
 
+    zeros = prolong([s["hand_v"][c] - co[A0, c] for c in range(3)], t)
+    twos = prolong([s["send_v"][c] - co[A2, c] for c in range(3)], t)
     for c in range(3):
-        zero = prolong(s["hand_v"][c] - co[A0, c], t)
-        two = prolong(s["send_v"][c] - co[A2, c], t)
+        zero, two = zeros[c], twos[c]
         for z in range(2):
             nodes[0, 0, c, z] = node[0, c, z] + zero[z]
             nodes[0, 1, c, z] = node[1, c, z] + 0.5 * (zero[z] + two[z])
@@ -894,7 +918,7 @@
 
     @pl.when(has_next)
     def _():
-        coarse_start(5)
+        end_start()
 
     slope = s["slope"]
     for c in range(3):
@@ -903,24 +927,16 @@
         for z in range(2):
             slope[c, z] = own[z] + (s["fh_low"][3, c, z] + s["fh_high"][3, c, z])
 
-    coarse_wait(5)
-    out = coarse_velocity(5)
-
-    change = [out[c] - co[UA2, c] for c in range(3)]
+    turned = restricted(lambda c, z: slope[c, z])
+    arrived(s["er"], s["c_rsem"].at[5])
+
+    out = along_both([s["er"][pl.ds(c, PARTS, stride=2 * COARSE), :] for c in range(6)], t, "ci_y")
+    change = [out[c] - co[UA2, c] for c in range(3)] + [out[3 + c] - turned[c] for c in range(3)]
+    put = prolong(change, t)
     for c in range(3):
-        s["ch_next"][4, c] = c_first_next(change[c])
-        s["ch_prev"][4, c] = c_first_prev(change[c])
-    begin(coarse_halo_copies(4))
-    for c in range(3):
-        put = prolong(change[c], t)
         for z in range(2):
-            speed[c, z] = speed[c, z] + put[z]
-    own = [c_first_own(change[c]) for c in range(3)]
-    landed(coarse_halo_copies(4))
-    for c in range(3):
-        put = prolong(own[c] + (s["ch_low"][4, c] + s["ch_high"][4, c]), t)
-        for z in range(2):
-            slope[c, z] = slope[c, z] + put[z]
+            speed[c, z] = speed[c, z] + put[c][z]
+            slope[c, z] = slope[c, z] + put[3 + c][z]
     for z in range(2):
         gx = [first_fine(speed[c, z], 0) for c in range(3)]
         gy = [first_fine(speed[c, z], 1) for c in range(3)]
@@ -933,15 +949,16 @@
         left(s["gs"].at[i], THIRD, s["g_ssem"].at[i], PARTS if i < 3 else PARTS - 1)
     for i in range(6):
         left(s["fs"].at[i], FINE, s["f_ssem"].at[i])
-    for i in (0, 1, 3, 4, 5):
+    for i in (0, 1, 3, 4):
         left(s["cs"].at[i], COARSE, s["c_ssem"].at[i])
+    left(s["es"], 2 * COARSE, s["c_ssem"].at[5])
 
     @pl.when(jnp.logical_not(is_first))
     def _():
         left(s["cs"].at[2], COARSE, s["c_ssem"].at[2])
         gone(coarse_halo_copies(2))
 
-    for i in range(4):
+    for i in (0, 1, 3):
         for c in range(3):
             gone(fine_halo(i, c))
     for i in (0, 1, 3, 4):

time: 228 us -> 223 us (0.978)
  Pallas kernels: 224 us -> 219 us
    pallas_call x1, Pallas kernels: 224 us -> 219 us  [body(): pl.pallas_call(kernel, out_shape=(jax.ShapeDtypeStruct((1, 3, 3, 2, N, N)...]
where the time goes in v3:
time: 223 us
  Pallas kernels  219 us (98%)
  local copies, waits for them, and re-layouts  3.08 us (1%)
    pallas_call x1, Pallas kernels, body(): pl.pallas_call(kernel, out_shape=(jax.ShapeDtypeStruct((1, 3, 3, 2, N, N)...  219 us

profile of v3, /device:TPU:24, one launch (start us, length us, event | category | flops | bytes accessed | tf_op | source)
XLA Modules:
  0.0 222.5 jit_solution(2831980147682948536)
XLA Ops:
  0.6 218.8 %shard_map.68 = (f32[1,3,3,2,128,128]{5,4,3,2,1,0:T(8,128)}, f32[1,2,128,128]{3,2,1,0:T(8,128)}) custom-call(f32[3,2,128,128]{3,2,1,0:T(8,128)} %refs_0_.1, f32[1,3,2,128,128]{4,3,2,1,0:T(8,128)} %refs_1_.1, f32[1,3,3,2,128,128]{5,4,3,2,1,0:T(8,128)} %refs_2_.1, f32[1368,128]{1,0:T(8,128)} %constant.4.clone.refs_3_, bf16[3968,256]{1,0:T(8,128)(2,1)} %constant.5.clone.refs_4_), custom_call_target="tpu_custom_call" | custom-call | tf_op jit(solution)/shard_map/pallas_call | solution.py:977
  219.4 0.0 copy-start
  219.5 2.4 %copy.9 = f32[1,3,3,2,128,128]{5,4,3,2,1,0:T(8,128)} copy(f32[1,3,3,2,128,128]{5,4,3,2,1,0:T(8,128)} %get-tuple-element.4) | data formatting | bytes 2359296
  221.9 0.0 copy-done
  221.9 0.7 copy.10
Async XLA Ops:
  219.4 2.4 %copy-start = (f32[1,2,128,128]{3,2,1,0:T(8,128)S(1)}, f32[1,2,128,128]{3,2,1,0:T(8,128)}, u32[]{:S(2)}) copy-start(f32[1,2,128,128]{3,2,1,0:T(8,128)} %get-tuple-element.5) | copy-start | bytes 393220

commit v4 on v3

--- a/solution.py
+++ b/solution.py
@@ -435,7 +435,7 @@
         z = 4 + ((j + 1) // 2) * (1 - 2 * lax.rem(j, 2))
         for x in (2, 1, 3, 0):
             for c in (1, 0):
-                greet(z, x, c, (up, down, row))
+                greet(z, x, c, (down, row))
         return carry
 
     for i in (0, 1, 4, 3, 2):
@@ -443,7 +443,7 @@
     lax.fori_loop(0, 7, greet_far, 0)
     for x in (2, 1, 3, 0):
         for c in (1, 0):
-            greet(0, x, c, (up, down, row) if x or c else (up, down))
+            greet(0, x, c, (down, row) if x or c else (down,))
     for i in (0, 1, 3, 4):
         loads[i].wait()
 
@@ -711,7 +711,7 @@
     for c in range(3):
         for z in range(2):
             fine_spread(c, z, jnp.where(has_next, end[0, c, z], init[c, z]))
-    pl.semaphore_wait(barrier, 3 * PARTS - 1)
+    pl.semaphore_wait(barrier, 2 * PARTS - 1)
 
     for m in range(3):
         if m == 0:
@@ -971,22 +971,43 @@
             copy.wait_send()
 
 
+def place(nodes, q, nodes_out, q_out, sems):
+    copies = [pltpu.make_async_copy(q, q_out, sems.at[9])]
+    for i in range(3):
+        for c in range(3):
+            copies.append(pltpu.make_async_copy(nodes.at[0, i, c], nodes_out.at[0, i, c], sems.at[3 * i + c]))
+    for copy in copies:
+        copy.start()
+    for copy in copies:
+        copy.wait()
+
+
 def body(initial_state, end_states, old_tendencies):
     vmem = pl.BlockSpec(memory_space=pltpu.VMEM)
     operands = [initial_state, end_states, old_tendencies, jnp.asarray(PACKED_32), jnp.asarray(PACKED_16)]
-    return pl.pallas_call(
+    shapes = (
+        jax.ShapeDtypeStruct((1, 3, 3, 2, N, N), f32),
+        jax.ShapeDtypeStruct((1, 2, N, N), f32),
+    )
+    anywhere = pl.BlockSpec(memory_space=pl.ANY)
+    results = pl.pallas_call(
         kernel,
-        out_shape=(
-            jax.ShapeDtypeStruct((1, 3, 3, 2, N, N), f32),
-            jax.ShapeDtypeStruct((1, 2, N, N), f32),
-        ),
-        in_specs=[pl.BlockSpec(memory_space=pl.ANY)] * len(operands),
+        out_shape=shapes,
+        in_specs=[anywhere] * len(operands),
         out_specs=(vmem, vmem),
         scratch_shapes=[pltpu.VMEM(x.shape, x.dtype) for x in operands] + list(SCRATCH.values()),
         compiler_params=pltpu.CompilerParams(
             collective_id=0, has_side_effects=True, vmem_limit_bytes=56 * 1024 * 1024
         ),
     )(*operands)
+    return pl.pallas_call(
+        place,
+        out_shape=shapes,
+        in_specs=[anywhere] * 2,
+        out_specs=(anywhere, anywhere),
+        scratch_shapes=[pltpu.SemaphoreType.DMA((10,))],
+        compiler_params=pltpu.CompilerParams(vmem_limit_bytes=63 * 1024 * 1024),
+    )(*results)
 
 
 def solution(mesh):

time: 223 us -> 261 us (1.17)
  Pallas kernels: 219 us -> 259 us
  local copies, waits for them, and re-layouts: 3.08 us -> 0 us
    pallas_call x1 -> x2, Pallas kernels: 219 us -> 259 us  [the longest x1 218 us: body(): pl.pallas_call(kernel, out_shape=shapes, in_specs=[anywhere] * len(operan...]
    unnamed x4 -> x0, local copies, waits for them, and re-layouts: 3.08 us -> none
where the time goes in v4:
time: 261 us; the launch traced here: 260 us
  Pallas kernels  259 us (99%)
    pallas_call x1, Pallas kernels, body(): pl.pallas_call(kernel, out_shape=shapes, in_specs=[anywhere] * len(operan...  218 us
    pallas_call x1, Pallas kernels, body(): pl.pallas_call(place, out_shape=shapes, in_specs=[anywhere] * 2, out_spec...  40.9 us

profile of v4, /device:TPU:24, one launch (start us, length us, event | category | flops | bytes accessed | tf_op | source)
XLA Modules:
  0.0 260.2 jit_solution(1790872051020693443)
XLA Ops:
  0.6 218.5 %shard_map.68 = (f32[1,3,3,2,128,128]{5,4,3,2,1,0:T(8,128)}, f32[1,2,128,128]{3,2,1,0:T(8,128)}) custom-call(f32[3,2,128,128]{3,2,1,0:T(8,128)} %refs_0_.1, f32[1,3,2,128,128]{4,3,2,1,0:T(8,128)} %refs_1_.1, f32[1,3,3,2,128,128]{5,4,3,2,1,0:T(8,128)} %refs_2_.1, f32[1368,128]{1,0:T(8,128)} %constant.4.clone.refs_3_, bf16[3968,256]{1,0:T(8,128)(2,1)} %constant.5.clone.refs_4_), custom_call_target="tpu_custom_call" | custom-call | tf_op jit(solution)/shard_map/pallas_call | solution.py:993
  219.1 40.9 %shard_map.69 = (f32[1,3,3,2,128,128]{5,4,3,2,1,0:T(8,128)}, f32[1,2,128,128]{3,2,1,0:T(8,128)}) custom-call(f32[1,3,3,2,128,128]{5,4,3,2,1,0:T(8,128)} %get-tuple-element.4.nodes, f32[1,2,128,128]{3,2,1,0:T(8,128)} %get-tuple-element.5.q), custom_call_target="tpu_custom_call" | custom-call | tf_op jit(solution)/shard_map/pallas_call | solution.py:1003
